TPU v7x, 32 devices: a whole 2x2x4 slice. The times are simulated.
32 devices in a mesh: dp: 8 (over z, y), fsdp: 4 (over x, core).
Axes of the slice: x: 2, y: 2, z: 4, core: 2. Of those that a mesh axis runs over, the one named last changes fastest.
Arguments:
- tokens: bfloat16 [12288, 768], P(('dp', 'fsdp')), may hold values from -6 to 6
- qkv_weight: bfloat16 [768, 2304], P(('dp', 'fsdp')), may hold values from -0.21875 to 0.21875
- out_weight: bfloat16 [768, 768], P(('dp', 'fsdp')), may hold values from -0.875 to 0.875
- up_weight: bfloat16 [768, 3072], P(('dp', 'fsdp')), may hold values from -0.21875 to 0.21875
- down_weight: bfloat16 [3072, 768], P(('dp', 'fsdp')), may hold values from -0.109375 to 0.109375
- norm_gains: bfloat16 [768, 2], P(('dp', 'fsdp')), may hold values from 0.5 to 1.5
- up_bias: bfloat16 [3072], P(('dp', 'fsdp')), may hold values from -3 to 3
- pass_table: bfloat16 [768, 5], P(('dp', 'fsdp')), may hold values from -3 to 3
- pass_index: int32 [2], replicated, may hold values from 0 to 4
- lengths: int32 [8], P('dp'), may hold values from 1153 to 1536, as said below
- cotangent: bfloat16 [12288, 768], P(('dp', 'fsdp')), may hold values from -6 to 6
Outputs:
- block_out: bfloat16 [12288, 768], P(('dp', 'fsdp'))
- input_grad: float32 [12288, 768], P(('dp', 'fsdp'))
- qkv_grad: float32 [768, 2304], P(('dp', 'fsdp'))
- out_grad: float32 [768, 768], P(('dp', 'fsdp'))
- up_grad: float32 [768, 3072], P(('dp', 'fsdp'))
- down_grad: float32 [3072, 768], P(('dp', 'fsdp'))
- gain_grad: float32 [768, 2], P(('dp', 'fsdp'))
- bias_grad: float32 [3072], P(('dp', 'fsdp'))
- table_grad: float32 [768, 5], P(('dp', 'fsdp'))
Inputs may be any that keep to these rules, and one draw needn't show every extreme that they name: `lengths`: every length is at least 1153, and some sequence has length exactly 1536.
All inputs are finite; a program needn't handle non-finite values.
Results may differ from a plain program's by a relative error of at most 0.013.
Values may be sent and summed in bfloat16 or wider, within the bound.
A program may use at most 192 MiB of HBM per device.

v0:
```python
from functools import partial

import jax
import jax.numpy as jnp
from jax import lax
from jax.sharding import PartitionSpec as P

HEADS = 12


def layer_norm(values, gain_vec):
    center = values - jnp.mean(values, axis=-1, keepdims=True)
    spread = jnp.mean(center * center, axis=-1, keepdims=True)
    return center * lax.rsqrt(spread + 1e-05) * gain_vec


def pair_slices(queries, context, group_index, head_width):
    model_width = queries.shape[1]
    pair_width = 2 * head_width
    query_pair = lax.dynamic_slice_in_dim(queries, group_index * pair_width, pair_width, 1)
    key_pair = lax.dynamic_slice_in_dim(context, group_index * pair_width, pair_width, 1)
    value_pair = lax.dynamic_slice_in_dim(
        context, model_width + group_index * pair_width, pair_width, 1
    )
    return (
        query_pair.reshape(queries.shape[0], 2, head_width),
        key_pair.reshape(context.shape[0], 2, head_width),
        value_pair.reshape(context.shape[0], 2, head_width),
    )


def pair_scores(query_pair, key_pair, allowed, head_width):
    scores = jnp.einsum(
        "qhd,khd->hqk", query_pair, key_pair, preferred_element_type=jnp.float32
    ) * head_width ** (-0.5)
    return jnp.where(allowed[None], scores, -1e30)


def side_by_side(stacked):
    return jnp.moveaxis(stacked, 0, 1).reshape(
        stacked.shape[1], stacked.shape[0] * stacked.shape[2]
    )


def attend_forward(queries, context, allowed, head_width):
    group_count = queries.shape[1] // (2 * head_width)

    def one_group(group_index):
        query_pair, key_pair, value_pair = pair_slices(queries, context, group_index, head_width)
        scores = pair_scores(query_pair, key_pair, allowed, head_width)
        highest = jnp.max(scores, axis=-1, keepdims=True)
        denominator = jnp.sum(jnp.exp(scores - highest), axis=-1, keepdims=True)
        log_total = highest + jnp.log(denominator)
        attend = jnp.exp(scores - log_total)
        mixed_rows = jnp.einsum(
            "hqk,khd->qhd",
            attend.astype(jnp.bfloat16),
            value_pair,
            preferred_element_type=jnp.float32,
        )
        return (mixed_rows.reshape(mixed_rows.shape[0], 2 * head_width), log_total[..., 0])

    mixed_rows, log_total = lax.map(one_group, jnp.arange(group_count, dtype=jnp.int32))
    return (side_by_side(mixed_rows), log_total)


def attend_backward(queries, context, allowed, head_width, log_total, grad_mixed):
    group_count = queries.shape[1] // (2 * head_width)
    scale = head_width ** (-0.5)

    def one_group(packed):
        group_index, log_part = packed
        query_pair, key_pair, value_pair = pair_slices(queries, context, group_index, head_width)
        grad_pair = lax.dynamic_slice_in_dim(
            grad_mixed, group_index * 2 * head_width, 2 * head_width, 1
        ).reshape(queries.shape[0], 2, head_width)
        scores = pair_scores(query_pair, key_pair, allowed, head_width)
        attend = jnp.exp(scores - log_part[..., None])
        grad_attend = jnp.einsum(
            "qhd,khd->hqk", grad_pair, value_pair, preferred_element_type=jnp.float32
        )
        inner_sum = jnp.sum(attend * grad_attend, axis=-1, keepdims=True)
        grad_scores = (attend * (grad_attend - inner_sum)).astype(jnp.bfloat16)
        grad_query = (
            jnp.einsum("hqk,khd->qhd", grad_scores, key_pair, preferred_element_type=jnp.float32)
            * scale
        )
        grad_key = (
            jnp.einsum("hqk,qhd->khd", grad_scores, query_pair, preferred_element_type=jnp.float32)
            * scale
        )
        grad_value = jnp.einsum(
            "hqk,qhd->khd",
            attend.astype(jnp.bfloat16),
            grad_pair,
            preferred_element_type=jnp.float32,
        )
        pair_width = 2 * head_width
        return (
            grad_query.reshape(-1, pair_width),
            grad_key.reshape(-1, pair_width),
            grad_value.reshape(-1, pair_width),
        )

    grad_query, grad_key, grad_value = lax.map(
        one_group, (jnp.arange(group_count, dtype=jnp.int32), log_total)
    )
    return (
        side_by_side(grad_query),
        jnp.concatenate([side_by_side(grad_key), side_by_side(grad_value)], axis=1),
    )


def pass_forward(stream, block_full, embedding, allowed, head_width):
    qkv_full, out_full, up_full, down_full, gain_full, bias_full = block_full[:6]
    model_width = stream.shape[1]
    hidden = stream + embedding[None, :]
    first_norm = layer_norm(hidden, gain_full[:, 0].astype(jnp.float32)).astype(jnp.bfloat16)
    qkv_rows = jnp.dot(first_norm, qkv_full, preferred_element_type=jnp.float32).astype(
        jnp.bfloat16
    )
    context = lax.all_gather(qkv_rows[:, model_width:], "fsdp", axis=0, tiled=True)
    mixed_rows, log_total = attend_forward(qkv_rows[:, :model_width], context, allowed, head_width)
    mixed_rows = mixed_rows.astype(jnp.bfloat16)
    after_attn = hidden + jnp.dot(mixed_rows, out_full, preferred_element_type=jnp.float32)
    second_norm = layer_norm(after_attn, gain_full[:, 1].astype(jnp.float32)).astype(jnp.bfloat16)
    pre_gelu = jnp.dot(second_norm, up_full, preferred_element_type=jnp.float32) + bias_full.astype(
        jnp.float32
    )
    active = jax.nn.gelu(pre_gelu, approximate=True).astype(jnp.bfloat16)
    result = after_attn + jnp.dot(active, down_full, preferred_element_type=jnp.float32)
    return (
        result,
        (
            hidden,
            first_norm,
            qkv_rows,
            context,
            mixed_rows,
            log_total,
            after_attn,
            second_norm,
            pre_gelu,
            active,
        ),
    )


def pass_backward(stream, block_full, embedding, chooser, allowed, head_width, grad_next):
    qkv_full, out_full, up_full, down_full, gain_full, bias_full = block_full[:6]
    model_width = stream.shape[1]
    result, kept_rows = pass_forward(stream, block_full, embedding, allowed, head_width)
    (
        hidden,
        first_norm,
        qkv_rows,
        context,
        mixed_rows,
        log_total,
        after_attn,
        second_norm,
        pre_gelu,
        active,
    ) = kept_rows
    grad_down_out = grad_next.astype(jnp.bfloat16)
    down_grad = jnp.einsum("ta,tb->ab", active, grad_down_out, preferred_element_type=jnp.float32)
    grad_active = jnp.einsum(
        "tb,ab->ta", grad_down_out, down_full, preferred_element_type=jnp.float32
    )
    unused_value, gelu_back = jax.vjp(partial(jax.nn.gelu, approximate=True), pre_gelu)
    grad_inner = gelu_back(grad_active)[0].astype(jnp.bfloat16)
    bias_grad = jnp.sum(grad_inner.astype(jnp.float32), axis=0)
    up_grad = jnp.einsum("ta,tb->ab", second_norm, grad_inner, preferred_element_type=jnp.float32)
    grad_second = jnp.einsum("tb,ab->ta", grad_inner, up_full, preferred_element_type=jnp.float32)
    unused_norm, norm_back_two = jax.vjp(
        layer_norm, after_attn, gain_full[:, 1].astype(jnp.float32)
    )
    grad_after_norm, gain_two = norm_back_two(grad_second)
    grad_after = grad_next + grad_after_norm
    grad_branch = grad_after.astype(jnp.bfloat16)
    out_grad = jnp.einsum("ta,tb->ab", mixed_rows, grad_branch, preferred_element_type=jnp.float32)
    grad_mixed = jnp.einsum(
        "tb,ab->ta", grad_branch, out_full, preferred_element_type=jnp.float32
    ).astype(jnp.bfloat16)
    grad_query, grad_context = attend_backward(
        qkv_rows[:, :model_width], context, allowed, head_width, log_total, grad_mixed
    )
    grad_local = lax.psum_scatter(
        grad_context.astype(jnp.bfloat16), "fsdp", scatter_dimension=0, tiled=True
    ).astype(jnp.float32)
    grad_qkv = jnp.concatenate([grad_query, grad_local], axis=1).astype(jnp.bfloat16)
    qkv_grad = jnp.einsum("ta,tb->ab", first_norm, grad_qkv, preferred_element_type=jnp.float32)
    grad_first = jnp.einsum("tb,ab->ta", grad_qkv, qkv_full, preferred_element_type=jnp.float32)
    unused_first, norm_back_one = jax.vjp(layer_norm, hidden, gain_full[:, 0].astype(jnp.float32))
    grad_hidden_norm, gain_one = norm_back_one(grad_first)
    grad_hidden = grad_after + grad_hidden_norm
    gain_grad = jnp.stack([gain_one, gain_two], axis=1)
    table_grad = jnp.sum(grad_hidden, axis=0)[:, None] * chooser[None, :]
    return (grad_hidden, (qkv_grad, out_grad, up_grad, down_grad, gain_grad, bias_grad, table_grad))


def body(
    tokens,
    qkv_weight,
    out_weight,
    up_weight,
    down_weight,
    norm_gains,
    up_bias,
    pass_table,
    pass_index,
    lengths,
    cotangent,
):
    row_count = tokens.shape[0]
    head_width = tokens.shape[1] // HEADS
    seq_len = row_count * lax.axis_size("fsdp")
    seq_limit = lengths[0]
    row_pos = lax.axis_index("fsdp") * row_count + jnp.arange(row_count, dtype=jnp.int32)
    key_pos = jnp.arange(seq_len, dtype=jnp.int32)
    allowed = (key_pos[None, :] <= row_pos[:, None]) & (key_pos[None, :] < seq_limit)
    valid_rows = (row_pos < seq_limit).astype(jnp.float32)[:, None]
    repeats = pass_table.shape[1]
    chooser = [
        (jnp.arange(repeats, dtype=jnp.int32) == pass_index[number]).astype(jnp.float32)
        for number in range(2)
    ]

    def embedding_of(block_full, number):
        return jnp.dot(
            block_full[6], chooser[number].astype(jnp.bfloat16), preferred_element_type=jnp.float32
        )

    def current_block():
        return (
            lax.all_gather(qkv_weight, ("dp", "fsdp"), axis=0, tiled=True),
            lax.all_gather(out_weight, ("dp", "fsdp"), axis=0, tiled=True),
            lax.all_gather(up_weight, ("dp", "fsdp"), axis=0, tiled=True),
            lax.all_gather(down_weight, ("dp", "fsdp"), axis=0, tiled=True),
            lax.all_gather(norm_gains, ("dp", "fsdp"), axis=0, tiled=True),
            lax.all_gather(up_bias, ("dp", "fsdp"), axis=0, tiled=True),
            lax.all_gather(pass_table, ("dp", "fsdp"), axis=0, tiled=True),
        )

    states = [tokens.astype(jnp.float32)]
    for number in range(2):
        block_full = current_block()
        result, unused_kept = pass_forward(
            states[number], block_full, embedding_of(block_full, number), allowed, head_width
        )
        states.append(result)
    block_out = (states[2] * valid_rows).astype(jnp.bfloat16)
    grad_stream = cotangent.astype(jnp.float32) * valid_rows
    running = None
    for number in (1, 0):
        block_full = current_block()
        grad_stream, gradients = pass_backward(
            states[number],
            block_full,
            embedding_of(block_full, number),
            chooser[number],
            allowed,
            head_width,
            grad_stream,
        )
        shares = (
            lax.psum_scatter(gradients[0], ("dp", "fsdp"), scatter_dimension=0, tiled=True),
            lax.psum_scatter(gradients[1], ("dp", "fsdp"), scatter_dimension=0, tiled=True),
            lax.psum_scatter(gradients[2], ("dp", "fsdp"), scatter_dimension=0, tiled=True),
            lax.psum_scatter(gradients[3], ("dp", "fsdp"), scatter_dimension=0, tiled=True),
            lax.psum_scatter(gradients[4], ("dp", "fsdp"), scatter_dimension=0, tiled=True),
            lax.psum_scatter(gradients[5], ("dp", "fsdp"), scatter_dimension=0, tiled=True),
            lax.psum_scatter(gradients[6], ("dp", "fsdp"), scatter_dimension=0, tiled=True),
        )
        running = shares if running is None else jax.tree.map(jnp.add, running, shares)
    return (
        block_out,
        grad_stream,
        running[0],
        running[1],
        running[2],
        running[3],
        running[4],
        running[5],
        running[6],
    )


def solution(mesh):
    placed = (
        P(("dp", "fsdp"), None),
        P(("dp", "fsdp"), None),
        P(("dp", "fsdp"), None),
        P(("dp", "fsdp"), None),
        P(("dp", "fsdp"), None),
        P(("dp", "fsdp"), None),
        P(("dp", "fsdp")),
        P(("dp", "fsdp"), None),
        P(),
        P("dp"),
        P(("dp", "fsdp"), None),
    )
    return jax.shard_map(
        body,
        mesh=mesh,
        in_specs=placed,
        out_specs=(
            P(("dp", "fsdp"), None),
            P(("dp", "fsdp"), None),
            P(("dp", "fsdp"), None),
            P(("dp", "fsdp"), None),
            P(("dp", "fsdp"), None),
            P(("dp", "fsdp"), None),
            P(("dp", "fsdp"), None),
            P(("dp", "fsdp")),
            P(("dp", "fsdp"), None),
        ),
        check_vma=False,
    )
```

profile of v0, /device:TPU:1, one launch (start us, length us, event | category | flops | bytes accessed | tf_op | source)
XLA Modules:
  0.0 1260.2 jit_solution(15020814991753211114)
XLA Ops:
  8.0 43.7 %all-gather = bf16[32,24,5]{1,2,0:T(8,128)(2,1)S(1)} all-gather(bf16[1,24,5]{1,2,0:T(8,128)(2,1)} %bitcast.371), channel_id=1, replica_groups=mesh['dp'=8,'fsdp'=4] {'dp','fsdp'}, dimensions={0}, use_global_device_ids=true | all-gather | bytes 7920 | tf_op jit(solution)/shard_map/all_gather | solution.py:242
  51.8 36.7 %all-gather.1 = bf16[32,24,2]{1,2,0:T(2,128)(2,1)S(1)} all-gather(bf16[1,24,2]{1,2,0:T(2,128)(2,1)} %bitcast.372), channel_id=1, replica_groups=mesh['dp'=8,'fsdp'=4] {'dp','fsdp'}, dimensions={0}, use_global_device_ids=true | all-gather | bytes 3168 | tf_op jit(solution)/shard_map/all_gather | solution.py:240
  102.2 36.1 %all-reduce = bf16[3072]{0:T(1024)(128)(2,1)S(1)} all-reduce(bf16[3072]{0:T(1024)(128)(2,1)S(1)} %dynamic-update-slice), channel_id=1, replica_groups=mesh['dp'=8,'fsdp'=4] {'dp','fsdp'}, use_global_device_ids=true, to_apply=%add | all-reduce | flops 3072 | bytes 12288
  145.4 35.9 %while.90 = (s32[]{:T(128)}, bf16[6,384,128]{1,2,0:T(8,128)(2,1)S(1)}, s32[6]{0:T(128)S(1)}, bf16[1536,1536]{0,1:T(8,128)(2,1)}, bf16[384,768]{0,1:T(8,128)(2,1)...) while((s32[]{:T(128)}, ...), condition=%wide.region_5.6_spmd.clone, body=%wide.region_2.5_spmd.clone.sunk | while | flops 311426304 | bytes 18309384 | solution.py:63
  181.3 9.5 all-gather.13.cloned.1.call-done
  193.3 62.8 %all-gather.17.cloned.1.call-done = bf16[3072,768]{1,0:T(8,128)(2,1)} async-done(((bf16[96,768]{1,0:T(8,128)(2,1)}), bf16[3072,768]{1,0:T(8,128)(2,1)}) %all-gather.17.cloned.1.call-update) | async-done | bytes 4718608 | tf_op jit(solution)/shard_map/all_gather | solution.py:239
  256.2 65.2 %all-gather.15.cloned.1.call-done = bf16[768,3072]{1,0:T(8,128)(2,1)} async-done(((bf16[24,3072]{1,0:T(8,128)(2,1)}), bf16[768,3072]{1,0:T(8,128)(2,1)}) %all-gather.15.cloned.1.call-update) | async-done | bytes 4718608 | tf_op jit(solution)/shard_map/all_gather | solution.py:238
  321.4 8.2 fusion.147
  336.4 34.7 %all-gather.19.cloned.1.call-done = bf16[1536,1536]{1,0:T(8,128)(2,1)} async-done(((bf16[384,1536]{1,0:T(8,128)(2,1)}), bf16[1536,1536]{1,0:T(8,128)(2,1)}) %all-gather.19.cloned.1.call-update) | async-done | bytes 4718608 | tf_op jit(solution)/shard_map/all_gather | solution.py:122
  378.6 44.8 %while.92 = (s32[]{:T(128)}, bf16[6,384,128]{1,2,0:T(8,128)(2,1)}, f32[6,2,384]{2,1,0:T(2,128)S(1)}, s32[6]{0:T(128)S(1)}, bf16[1536,1536]{0,1:T(8,128)(2,1)}, /...) while((s32[]{:T(128)}, bf16[6,384,128]{1,2,0:T(8,128)(2,1)}, ...), condition=%wide.region_19.20_spmd.clone, body=%wide.region_16.19_spmd.clone.sunk | while | flops 311426304 | bytes 18312468 | solution.py:63
  430.4 6.7 convert_reduce_fusion.1
  445.6 69.7 %while.93 = (s32[]{:T(128)}, bf16[6,384,128]{1,2,0:T(8,128)(2,1)S(1)}, bf16[6,1536,128]{1,2,0:T(8,128)(2,1)}, bf16[6,1536,128]{1,2,0:T(8,128)(2,1)}, s32[6]{0:T(...) while((s32[]{:T(128)}, ...), condition=%wide.region_26.27_spmd.clone, body=%wide.region_24.26_spmd.clone.sunk | while | flops 767261952 | bytes 42977588 | solution.py:105
  520.3 6.7 copy.66
  527.9 44.8 %while.94 = (s32[]{:T(128)}, bf16[6,384,128]{1,2,0:T(8,128)(2,1)}, f32[6,2,384]{2,1,0:T(2,128)S(1)}, s32[6]{0:T(128)S(1)}, bf16[1536,1536]{0,1:T(8,128)(2,1)}, /...) while((s32[]{:T(128)}, bf16[6,384,128]{1,2,0:T(8,128)(2,1)}, ...), condition=%wide.region_33.34_spmd.clone, body=%wide.region_30.33_spmd.clone.sunk | while | flops 311426304 | bytes 18312468 | solution.py:63
  594.0 8.8 convert_reduce_fusion
  612.5 69.7 %while.95 = (s32[]{:T(128)}, bf16[6,384,128]{1,2,0:T(8,128)(2,1)S(1)}, bf16[6,1536,128]{1,2,0:T(8,128)(2,1)}, bf16[6,1536,128]{1,2,0:T(8,128)(2,1)}, s32[6]{0:T(...) while((s32[]{:T(128)}, ...), condition=%wide.region_40.41_spmd.clone, body=%wide.region_38.40_spmd.clone.sunk | while | flops 767261952 | bytes 42977588 | solution.py:105
  718.1 9.2 convolution_add_fusion.1
  743.3 8.6 convolution_add_fusion
  752.9 55.3 %while.91 = (s32[]{:T(128)}, bf16[6,384,128]{1,2,0:T(8,128)(2,1)}, s32[6]{0:T(128)S(1)}, bf16[1536,1536]{0,1:T(8,128)(2,1)}, bf16[384,768]{0,1:T(8,128)(2,1)}, /...) while((s32[]{:T(128)}, bf16[6,384,128]{1,2,0:T(8,128)(2,1)}, ...), condition=%wide.region_13.14_spmd.clone, body=%wide.region_10.13_spmd.clone.sunk | while | flops 311426304 | bytes 18309384 | solution.py:63
  811.2 9.6 fusion.71
  827.6 39.3 %all-reduce.4 = (f32[768,2]{0,1:T(2,128)S(1)}, f32[3072]{0:T(1024)S(1)}, f32[768,5]{0,1:T(8,128)S(1)}) all-reduce(f32[768,2]{0,1:T(2,128)S(1)} %maximum_add_fusion, f32[3072]{0:T(1024)S(1)} %add.537, f32[768,5]{0,1:T(8,128)S(1)} %multiply_add_fusion), channel_id=15, replica_groups=mesh['dp'=8,'fsdp'=4] {'dp','fsdp'}, use_global_device_ids=true, to_apply=%region_54.55.clone | all-reduce | flops 8448 | bytes 67584
  868.8 118.0 %reduce-scatter.17.cloned.1.call-done = f32[24,3072]{1,0:T(8,128)} async-done(((f32[768,3072]{1,0:T(8,128)}), f32[24,3072]{1,0:T(8,128)}) %reduce-scatter.17.cloned.1.call-update) | async-done | bytes 294928 | tf_op jit(solution)/shard_map/reduce_scatter | solution.py:269
  986.8 141.0 %reduce-scatter.19.cloned.1.call-done = f32[96,768]{1,0:T(8,128)} async-done(((f32[3072,768]{1,0:T(8,128)}), f32[96,768]{1,0:T(8,128)}) %reduce-scatter.19.cloned.1.call-update) | async-done | bytes 294928 | tf_op jit(solution)/shard_map/reduce_scatter | solution.py:270
  1127.8 125.3 %reduce-scatter.13.cloned.1.call-done = f32[24,2304]{1,0:T(8,128)} async-done(((f32[768,2304]{1,0:T(8,128)}), f32[24,2304]{1,0:T(8,128)}) %reduce-scatter.13.cloned.1.call-update) | async-done | bytes 221200 | tf_op jit(solution)/shard_map/reduce_scatter | solution.py:267
  (726 shorter events, 447.7 us)
Async XLA Ops:
  7.2 86.3 %all-gather.9.cloned.1.call-start = ((), (), s32[]{:S(2)}) async-start(), calls=%async_computation.6 | async-start | bytes 3649536 | tf_op jit(solution)/shard_map/all_gather | solution.py:236
  7.9 130.8 %all-gather.11.cloned.1.call-start = ((), (), s32[]{:S(2)}) async-start(), calls=%async_computation.7 | async-start | bytes 5898240 | tf_op jit(solution)/shard_map/all_gather | solution.py:122
  90.7 100.1 %copy-start.39 = (f32[768]{0:T(1024)}, f32[768]{0:T(1024)S(1)}, u32[]{:S(2)}) copy-start(f32[768]{0:T(1024)S(1)} %convolution_reduce_fusion.1) | copy-start | bytes 9220
  90.8 239.2 %copy-start.37 = (f32[768]{0:T(1024)}, f32[768]{0:T(1024)S(1)}, u32[]{:S(2)}) copy-start(f32[768]{0:T(1024)S(1)} %get-tuple-element.904) | copy-start | bytes 9220
  98.5 92.4 %all-gather.13.cloned.1.call-start = ((), (), s32[]{:S(2)}) async-start(), calls=%async_computation.8 | async-start | bytes 1216512 | tf_op jit(solution)/shard_map/all_gather | solution.py:237
  99.2 156.9 %all-gather.17.cloned.1.call-start = ((), (), s32[]{:S(2)}) async-start(), calls=%async_computation.10 | async-start | bytes 4866048 | tf_op jit(solution)/shard_map/all_gather | solution.py:239
  99.8 221.6 %all-gather.15.cloned.1.call-start = ((), (), s32[]{:S(2)}) async-start(), calls=%async_computation.9 | async-start | bytes 4866048 | tf_op jit(solution)/shard_map/all_gather | solution.py:238
  100.4 270.7 %all-gather.19.cloned.1.call-start = ((), (), s32[]{:S(2)}) async-start(), calls=%async_computation.11 | async-start | bytes 5898240 | tf_op jit(solution)/shard_map/all_gather | solution.py:122
  138.3 183.1 %copy-start.74 = (f32[3072]{0:T(1024)}, f32[3072]{0:T(1024)S(1)}, u32[]{:S(2)}) copy-start(f32[3072]{0:T(1024)S(1)} %convert_element_type.247) | copy-start | bytes 36868
  145.4 45.5 %copy-start = (bf16[384,768]{1,0:T(8,128)(2,1)S(1)}, bf16[384,768]{1,0:T(8,128)(2,1)}, u32[]{:S(2)}) copy-start(bf16[384,768]{1,0:T(8,128)(2,1)} %param.23) | copy-start | bytes 1769476
  334.7 249.1 %reduce-scatter.21.cloned.1.call-start = ((), (), s32[]{:S(2)}) async-start(), calls=%async_computation.16 | async-start | bytes 5898240
  335.2 105.2 %copy-start.62 = (f32[384]{0:T(512)}, f32[384]{0:T(512)S(1)}, u32[]{:S(2)}) copy-start(f32[384]{0:T(512)S(1)} %compare_convert_fusion) | copy-start | bytes 4612
  378.6 44.8 %copy-start.12 = (bf16[768,768]{1,0:T(8,128)(2,1)S(1)}, bf16[768,768]{1,0:T(8,128)(2,1)}, u32[]{:S(2)}) copy-start(bf16[768,768]{1,0:T(8,128)(2,1)} %all-gather.13.cloned.1.call-done) | copy-start | bytes 3538948
  515.3 70.9 %copy-start.23 = (bf16[6,384,128]{1,2,0:T(8,128)(2,1)}, bf16[6,384,128]{1,2,0:T(8,128)(2,1)S(1)}, u32[]{:S(2)}) copy-start(bf16[6,384,128]{1,2,0:T(8,128)(2,1)S(1)} %get-tuple-element.603) | copy-start | bytes 1769476
  527.0 214.6 %reduce-scatter.23.cloned.1.call-start = ((), (), s32[]{:S(2)}) async-start(), calls=%async_computation.17 | async-start | bytes 5898240
  527.9 45.4 %copy-start.1 = (bf16[384,768]{1,0:T(8,128)(2,1)S(1)}, bf16[384,768]{1,0:T(8,128)(2,1)}, u32[]{:S(2)}) copy-start(bf16[384,768]{1,0:T(8,128)(2,1)} %param.23) | copy-start | bytes 1769476
  527.9 45.4 %copy-start.40 = (f32[768]{0:T(1024)S(1)}, f32[768]{0:T(1024)}, u32[]{:S(2)}) copy-start(f32[768]{0:T(1024)} %copy-done.39) | copy-start | bytes 9220
  575.6 29.9 %copy-start.8 = (f32[384,768]{1,0:T(8,128)}, f32[384,768]{1,0:T(8,128)S(1)}, u32[]{:S(2)}) copy-start(f32[384,768]{1,0:T(8,128)S(1)} %get-tuple-element.1067) | copy-start | bytes 3538948
  693.9 174.9 %reduce-scatter.15.cloned.1.call-start = ((), (), s32[]{:S(2)}) async-start(), calls=%async_computation.13 | async-start | bytes 2433024 | tf_op jit(solution)/shard_map/reduce_scatter | solution.py:268
  699.1 287.7 %reduce-scatter.17.cloned.1.call-start = ((), (), s32[]{:S(2)}) async-start(), calls=%async_computation.14 | async-start | bytes 9732096 | tf_op jit(solution)/shard_map/reduce_scatter | solution.py:269
  711.4 416.4 %reduce-scatter.19.cloned.1.call-start = ((), (), s32[]{:S(2)}) async-start(), calls=%async_computation.15 | async-start | bytes 9732096 | tf_op jit(solution)/shard_map/reduce_scatter | solution.py:270
  727.3 525.8 %reduce-scatter.13.cloned.1.call-start = ((), (), s32[]{:S(2)}) async-start(), calls=%async_computation.12 | async-start | bytes 7299072 | tf_op jit(solution)/shard_map/reduce_scatter | solution.py:267
  752.9 55.4 %copy-start.80 = (f32[768]{0:T(1024)S(1)}, f32[768]{0:T(1024)}, u32[]{:S(2)}) copy-start(f32[768]{0:T(1024)} %get-tuple-element.899) | copy-start | bytes 9220
  752.9 55.4 %copy-start.14 = (bf16[768,768]{1,0:T(8,128)(2,1)S(1)}, bf16[768,768]{1,0:T(8,128)(2,1)}, u32[]{:S(2)}) copy-start(bf16[768,768]{1,0:T(8,128)(2,1)} %all-gather.13.cloned.1.call-done) | copy-start | bytes 3538948
  (81 other events, 406.1 us)
Sparse Core Ops, SparseCore 0:
  10.9 62.6 all-gather.8
  98.6 35.4 all-gather.10
  137.1 53.7 all-gather.12
  193.6 62.5 all-gather.16
  258.9 62.4 all-gather.14
  334.8 36.2 all-gather.18
  527.1 47.4 reduce-scatter.20
  694.0 47.5 reduce-scatter.22
  747.5 97.4 reduce-scatter.14
  852.3 134.4 reduce-scatter.16
  993.3 134.4 reduce-scatter.18
  1134.8 118.2 reduce-scatter.12
where the time goes:
time: 1270 us; the launch traced here: 1260 us
  waiting for transfers between devices  565 us (44%)
  matrix products  236 us (19%)
  local copies, waits for them, and re-layouts  196 us (15%)
  blocking collectives  156 us (12%)
  other arithmetic  63.4 us (5%)
  loops' own time  25.9 us (2%)
  between operations  16.3 us (1%)
    reduce_scatter x1, waiting for transfers between devices, body(): lax.psum_scatter(gradients[3], ('dp', 'fsdp'), scatter_dimension=0, tiled...  141 us
    reduce_scatter x1, waiting for transfers between devices, body(): lax.psum_scatter(gradients[0], ('dp', 'fsdp'), scatter_dimension=0, tiled...  125 us
    reduce_scatter x1, waiting for transfers between devices, body(): lax.psum_scatter(gradients[2], ('dp', 'fsdp'), scatter_dimension=0, tiled...  118 us
    unnamed x2, blocking collectives  75.4 us
    all_gather x1, waiting for transfers between devices, current_block(): lax.all_gather(up_weight, ('dp', 'fsdp'), axis=0, tiled=True)  65.2 us
    all_gather x1, waiting for transfers between devices, current_block(): lax.all_gather(down_weight, ('dp', 'fsdp'), axis=0, tiled=True)  62.8 us
    dot_general x36, matrix products, pair_scores(): jnp.einsum('qhd,khd->hqk', query_pair, key_pair, preferred_element_type=j...  57.2 us
    unnamed x201, local copies, waits for them, and re-layouts  43.7 us
  transfers between devices with their start and end apart: 12, of which 8 were waited for; matrix products, arithmetic and copies ran while one was open for 17% of the time, Pallas kernels for 0%

commit v1 on v0

v1 whole, which is shorter than its diff:
```python
from functools import partial
import jax
import jax.numpy as jnp
from jax import lax
from jax.experimental import pallas as pl
from jax.experimental.pallas import tpu as pltpu
from jax.sharding import PartitionSpec as P
BF=jnp.bfloat16; F32=jnp.float32
MESH = pl.DeviceIdType.MESH
NEG = -1e30
QB = 512
VMEM_LIMIT = 58 * 2**20

def remote(src, dst, ssem, rsem, dev):
    return pltpu.make_async_remote_copy(src_ref=src, dst_ref=dst, send_sem=ssem, recv_sem=rsem, device_id=dev, device_id_type=MESH)

def rows_at(start, count, step=16):
    return pl.ds(pl.multiple_of(start, step), count)

def normed(values):
    center = values - jnp.mean(values, axis=-1, keepdims=True)
    spread = jnp.mean(center * center, axis=-1, keepdims=True)
    scale = lax.rsqrt(spread + 1e-05)
    return center * scale, scale

def norm_back(xhat, scale, grad_out, gain):
    eg = grad_out * gain
    first = jnp.mean(eg, axis=-1, keepdims=True)
    second = jnp.mean(eg * xhat, axis=-1, keepdims=True)
    return scale * (eg - first - xhat * second)

def nt(left, right):
    return lax.dot_general(left, right, (((1,), (1,)), ((), ())), preferred_element_type=F32)

def dot(left, right):
    return jnp.dot(left, right, preferred_element_type=F32)

def mask_scores(sT, i, limit):
    lo = i * QB
    free = min(lo, 1024)
    parts = []
    if free: parts.append(sT[:free])
    if lo > free:
        kpos = free + lax.broadcasted_iota(jnp.int32, (lo - free, QB), 0)
        parts.append(jnp.where(kpos < limit, sT[free:lo], NEG))
    kpos = lo + lax.broadcasted_iota(jnp.int32, (QB, QB), 0)
    ok = kpos <= lo + lax.broadcasted_iota(jnp.int32, (QB, QB), 1)
    if lo + QB > 1024: ok = ok & (kpos < limit)
    parts.append(jnp.where(ok, sT[lo:], NEG))
    return parts[0] if len(parts) == 1 else jnp.concatenate(parts, 0)

def pick(xT, h):
    r = lax.broadcasted_iota(jnp.int32, xT.shape, 0)
    return jnp.where((r // 64) == (h % 2), xT, jnp.zeros_like(xT))

def slot_of(h, base=0):
    return pl.ds(pl.multiple_of(base + (h // 2) * 128, 128), 128)

def fwd_block(i, qkv, limit, qT, vT, oT, lse):
    keys = (i + 1) * QB
    cols = pl.ds(i * QB, QB)
    def head(h, _):
        hr = pl.ds(pl.multiple_of(h * 64, 64), 64)
        sT = dot(qkv[0:keys, slot_of(h, 256)], pick(qT[slot_of(h), cols], h))
        sT = mask_scores(sT, i, limit)
        m = jnp.max(sT, axis=0, keepdims=True)
        p = jnp.exp(sT - m)
        l = jnp.sum(p, axis=0, keepdims=True)
        oT[hr, cols] = dot(vT[hr, 0:keys], p.astype(BF)) * (1.0 / l)
        lse[pl.ds(h, 1), cols] = m + jnp.log(l)
        return 0
    lax.fori_loop(0, 3, head, 0)

def bwd_block(i, qkv, do, lse, limit, qT, kT, doT, dqT, delta, dkv):
    keys = (i + 1) * QB
    cols = pl.ds(i * QB, QB)
    def head(h, _):
        hr = pl.ds(pl.multiple_of(h * 64, 64), 64)
        lm = (lax.broadcasted_iota(jnp.int32, (QB, 128), 1) // 64) == (h % 2)
        sT = dot(qkv[0:keys, slot_of(h, 256)], pick(qT[slot_of(h), cols], h))
        sT = mask_scores(sT, i, limit)
        p = jnp.exp(sT - lse[pl.ds(h, 1), cols])
        dp = dot(qkv[0:keys, slot_of(h, 512)], pick(doT[slot_of(h), cols], h))
        dsT = (p * (dp - delta[pl.ds(h, 1), cols])).astype(BF)
        dqT[hr, cols] = dot(kT[hr, 0:keys], dsT)
        qn = qkv[cols, slot_of(h)]
        dn = do[cols, slot_of(h)]
        dkv[0:keys, slot_of(h)] += dot(dsT, jnp.where(lm, qn, jnp.zeros_like(qn)))
        dkv[0:keys, slot_of(h, 256)] += dot(p.astype(BF), jnp.where(lm, dn, jnp.zeros_like(dn)))
        return 0
    lax.fori_loop(0, 3, head, 0)

def group_barrier(d, f):
    bar = pltpu.get_barrier_semaphore()
    for k in (1, 2, 3):
        pl.semaphore_signal(bar, inc=1, device_id=(d, f ^ k), device_id_type=MESH)
    pl.semaphore_wait(bar, 3)

T, D, FF, S = 384, 768, 3072, 1536
CH = 128

def fwd_kernel(lim, x, vec, bias, wq_h, wou_h, wd_h,
               xo_h, n1_h, qkv_h, o_h, lse_h, og_h, r_h, n2_h, gp_h, a_h,
               wq, wou, wd, n1, qkv, qT, vT, oT, o, lse, og, r, n2, gp, a, xo,
               lsem, osem, ssem, rsem):
    d = lax.axis_index("dp"); f = lax.axis_index("fsdp")
    loads = [pltpu.make_async_copy(s, t, lsem.at[i]) for i, (s, t) in enumerate([(wq_h, wq), (wou_h, wou), (wd_h, wd)])]
    for c in loads: c.start()
    group_barrier(d, f)
    stores = []
    def store(src, dst):
        c = pltpu.make_async_copy(src, dst, osem.at[len(stores)])
        c.start(); stores.append(c)
    limit = lim[0]
    g0, g1, emb = vec[0:1, :], vec[1:2, :], vec[2:3, :]
    sends = []
    def send(src, dst, k, dev):
        c = remote(src, dst, ssem.at[k], rsem.at[k], dev)
        c.start(); sends.append(c)
    def got(region, k):
        remote(region, region, ssem.at[k], rsem.at[k], (d, f ^ 1)).wait_recv()
    for j in range(T // CH):
        rows = pl.ds(j * CH, CH)
        xhat, _ = normed(x[rows, :].astype(F32) + emb)
        n1[f, rows, :] = (xhat * g0).astype(BF)
        reg = n1.at[f, rows, :]
        send(reg, reg, j, (d, f ^ 2))
        send(reg, reg, 3 + j, (d, f ^ 1))
    loads[0].wait()
    def project(k):
        def tile(j, _):
            rows = rows_at(j * 192, 192)
            qkv[rows_at(k * T + j * 192, 192), :] = dot(n1[k, rows, :], wq[...]).astype(BF)
            return 0
        lax.fori_loop(0, 2, tile, 0)
    project(f)
    for j in range(3): got(n1.at[f ^ 1, pl.ds(j * CH, CH), :], 3 + j)
    project(f ^ 1)
    for j in range(3):
        reg = n1.at[f ^ 2, pl.ds(j * CH, CH), :]
        got(reg, j)
        send(reg, reg, 6 + j, (d, f ^ 1))
    project(f ^ 2)
    for j in range(3): got(n1.at[f ^ 3, pl.ds(j * CH, CH), :], 6 + j)
    project(f ^ 3)
    store(n1, n1_h); store(qkv, qkv_h)
    qT[...] = (qkv[:, 0:256] * 0.125).astype(BF).T
    vT[...] = qkv[:, 512:768].T
    oT[192:256, :] = jnp.zeros((64, S), F32)
    lse[...] = jnp.zeros_like(lse)
    def finish(b):
        rows = pl.ds(b * T, T)
        o[rows, :] = oT[:, rows].astype(BF).T
        @pl.when(f == b)
        def _(): og[b] = o[rows, :]
        for k in (1, 2, 3):
            @pl.when((f ^ k) == b)
            def _(): remote(o.at[rows, :], og.at[f], ssem.at[8 + k], rsem.at[8 + k], (d, f ^ k)).start()
    for i in reversed(range(S // QB)):
        fwd_block(i, qkv, limit, qT, vT, oT, lse)
        for b in reversed(range(4)):
            if i * QB <= b * T and not (b * T >= (i + 1) * QB): finish(b)
    store(o, o_h); store(lse, lse_h)
    for k in (1, 2, 3): got(og.at[f ^ k], 8 + k)
    store(og, og_h)
    loads[1].wait()
    def out_rows(j, _):
        rows = rows_at(j * 192, 192)
        acc = x[rows, :].astype(F32) + emb
        for k in range(4):
            acc = acc + dot(og[k, rows, 0:192], wou[k * 192:(k + 1) * 192, 0:D])
        r[rows, :] = acc
        xhat, _ = normed(acc)
        n2[rows, :] = (xhat * g1).astype(BF)
        return 0
    lax.fori_loop(0, 2, out_rows, 0)
    store(r, r_h); store(n2, n2_h)
    W = 768
    def up_tile(j, _):
        cols = pl.ds(pl.multiple_of(j * W, 128), W)
        u = dot(n2[...], wou[:, pl.ds(pl.multiple_of(D + j * W, 128), W)]) + bias[:, cols]
        sq = u * u
        t = jnp.tanh(0.7978845608028654 * u * (1.0 + 0.044715 * sq))
        half = 0.5 * (1.0 + t)
        a[:, cols] = (u * half).astype(BF)
        gp[:, cols] = (half + 0.5 * u * (1.0 - t * t) * (0.7978845608028654 * (1.0 + 0.134145 * sq))).astype(BF)
        return 0
    lax.fori_loop(0, FF // W, up_tile, 0)
    store(gp, gp_h); store(a, a_h)
    loads[2].wait()
    def down_tile(j, _):
        cols = pl.ds(pl.multiple_of(j * 256, 128), 256)
        xo[:, cols] = r[:, cols] + dot(a[...], wd[:, cols])
        return 0
    lax.fori_loop(0, D // 256, down_tile, 0)
    store(xo, xo_h)
    for c in sends: c.wait_send()
    for k in (1, 2, 3): remote(o.at[pl.ds(0, T), :], og.at[f], ssem.at[8 + k], rsem.at[8 + k], (d, f ^ k)).wait_send()
    for c in stores: c.wait()

def fwd(lim, x, vec, bias, wq, wou, wd, cid):
    Z = jax.ShapeDtypeStruct
    hbm = pl.BlockSpec(memory_space=pltpu.HBM); vm = pl.BlockSpec(memory_space=pltpu.VMEM); sm = pl.BlockSpec(memory_space=pltpu.SMEM)
    V = pltpu.VMEM
    outs = [((T, D), F32), ((4, T, D), BF), ((S, D), BF), ((S, 256), BF), ((8, S), F32), ((4, T, 256), BF), ((T, D), F32), ((T, D), BF), ((T, FF), BF), ((T, FF), BF)]
    return pl.pallas_call(fwd_kernel, out_shape=[Z(*s) for s in outs],
        in_specs=[sm, vm, vm, vm, hbm, hbm, hbm], out_specs=[hbm] * len(outs),
        scratch_shapes=[V((D, D), BF), V((D, 3840), BF), V((FF, D), BF), V((4, T, D), BF), V((S, D), BF), V((256, S), BF), V((256, S), BF), V((256, S), F32),
            V((S, 256), BF), V((8, S), F32), V((4, T, 256), BF), V((T, D), F32), V((T, D), BF), V((T, FF), BF), V((T, FF), BF), V((T, D), F32),
            pltpu.SemaphoreType.DMA((3,)), pltpu.SemaphoreType.DMA((16,)), pltpu.SemaphoreType.DMA((12,)), pltpu.SemaphoreType.DMA((12,))],
        compiler_params=pltpu.CompilerParams(collective_id=cid, has_side_effects=True, vmem_limit_bytes=VMEM_LIMIT))(lim, x, vec, bias, wq, wou, wd)

def bwd_kernel(lim, g, x, vec, wq_h, wou_h, wd_h, qkv_h, o_h, lse_h, r_h, gp_h,
               go_h, dm_h, du_h, da_h, dqkv_h, sums, bsum,
               wq, wou, wd, qkv, o, lse, r, gp, dm, du, da, dr, dos, do, qT, kT, doT, dqT, delta, dkv, dqkv, mine, part, inc, go,
               lsem, osem, ssem, rsem):
    d = lax.axis_index("dp"); f = lax.axis_index("fsdp")
    loads = [pltpu.make_async_copy(s, t, lsem.at[i]) for i, (s, t) in enumerate(
        [(wd_h, wd), (gp_h, gp), (wou_h, wou), (r_h, r), (qkv_h, qkv), (o_h, o), (lse_h, lse), (wq_h, wq)])]
    for c in loads: c.start()
    group_barrier(d, f)
    stores = []
    def store(src, dst):
        c = pltpu.make_async_copy(src, dst, osem.at[len(stores)])
        c.start(); stores.append(c)
    limit = lim[0]
    g0, g1, emb = vec[0:1, :], vec[1:2, :], vec[2:3, :]
    sends = []
    def send(src, dst, k, dev):
        c = remote(src, dst, ssem.at[k], rsem.at[k], dev)
        c.start(); sends.append(c)
    def got(region, k):
        remote(region, region, ssem.at[k], rsem.at[k], (d, f ^ 1)).wait_recv()
    dm[...] = g[...].astype(BF)
    store(dm, dm_h)
    loads[0].wait(); loads[1].wait()
    W = 768
    def up_tile(j, _):
        cols = pl.ds(pl.multiple_of(j * W, 128), W)
        t = (nt(dm[...], wd[cols, :]) * gp[:, cols].astype(F32)).astype(BF)
        du[:, cols] = t
        bsum[:, cols] = jnp.sum(t.astype(F32), axis=0, keepdims=True)
        return 0
    lax.fori_loop(0, FF // W, up_tile, 0)
    store(du, du_h)
    loads[2].wait(); loads[3].wait()
    sums[...] = jnp.zeros_like(sums)
    def norm2(j, _):
        rows = rows_at(j * 128, 128)
        e = nt(du[rows, :], wou[:, D:])
        xhat, scale = normed(r[rows, :])
        sums[1:2, :] += jnp.sum(e * xhat, axis=0, keepdims=True)
        t = g[rows, :] + norm_back(xhat, scale, e, g1)
        dr[rows, :] = t
        da[rows, :] = t.astype(BF)
        return 0
    lax.fori_loop(0, T // 128, norm2, 0)
    store(da, da_h)
    for k in (3, 2, 1, 0):
        b = f ^ k
        dos[b, :, 0:192] = nt(da[...], wou[rows_at(b * 192, 192), 0:D]).astype(BF)
        dos[b, :, 192:256] = jnp.zeros((T, 64), BF)
        if k:
            send(dos.at[b], do.at[rows_at(f * T, T), :], k, (d, b))
        else:
            do[rows_at(f * T, T), :] = dos[b]
    for c in loads[4:]: c.wait()
    qT[...] = (qkv[:, 0:256] * 0.125).astype(BF).T
    kT[...] = qkv[:, 256:512].T
    dqT[192:256, :] = jnp.zeros((64, S), F32)
    dkv[...] = jnp.zeros_like(dkv)
    for k in (1, 2, 3): got(do.at[rows_at((f ^ k) * T, T), :], k)
    doT[...] = do[...].T
    prod = (do[...].astype(F32) * o[...].astype(F32)).T
    for h in range(3):
        delta[h:h + 1, :] = jnp.sum(prod[h * 64:h * 64 + 64], axis=0, keepdims=True)
    for i in range(S // QB):
        bwd_block(i, qkv, do, lse, limit, qT, kT, doT, dqT, delta, dkv)
    dqkv[:, 0:256] = (dqT[...] * 0.125).astype(BF).T
    dqkv[:, 256:512] = (dkv[:, 0:256] * 0.125).astype(BF)
    dqkv[:, 512:768] = dkv[:, 256:512].astype(BF)
    store(dqkv, dqkv_h)
    def partial_rows(b, j):
        return nt(dqkv[rows_at(b * T + j * CH, CH), :], wq[...])
    for j in range(3):
        rows = pl.ds(j * CH, CH)
        mine[0, rows, :] = partial_rows(f ^ 3, j).astype(BF)
        send(mine.at[0, rows, :], part.at[0, rows, :], 4 + j, (d, f ^ 1))
    for j in range(3):
        rows = pl.ds(j * CH, CH)
        t = partial_rows(f ^ 2, j)
        got(part.at[0, rows, :], 4 + j)
        inc[rows, :] = (t + part[0, rows, :].astype(F32)).astype(BF)
        send(inc.at[rows, :], part.at[2, rows, :], 7 + j, (d, f ^ 2))
    for j in range(3):
        rows = pl.ds(j * CH, CH)
        mine[1, rows, :] = partial_rows(f ^ 1, j).astype(BF)
        send(mine.at[1, rows, :], part.at[1, rows, :], 10 + j, (d, f ^ 1))
    for j in range(3):
        rows = pl.ds(j * CH, CH)
        go[rows, :] = partial_rows(f, j)
    for j in range(3):
        rows = pl.ds(j * CH, CH)
        got(part.at[1, rows, :], 10 + j)
        got(part.at[2, rows, :], 7 + j)
        e = go[rows, :] + part[1, rows, :].astype(F32) + part[2, rows, :].astype(F32)
        xhat, scale = normed(x[rows, :].astype(F32) + emb)
        sums[0:1, :] += jnp.sum(e * xhat, axis=0, keepdims=True)
        t = dr[rows, :] + norm_back(xhat, scale, e, g0)
        sums[2:3, :] += jnp.sum(t, axis=0, keepdims=True)
        go[rows, :] = t
    store(go, go_h)
    for c in sends: c.wait_send()
    for c in stores: c.wait()

def bwd(lim, g, x, vec, wq, wou, wd, qkv, o, lse, r, gp, cid):
    Z = jax.ShapeDtypeStruct
    hbm = pl.BlockSpec(memory_space=pltpu.HBM); vm = pl.BlockSpec(memory_space=pltpu.VMEM); sm = pl.BlockSpec(memory_space=pltpu.SMEM)
    V = pltpu.VMEM
    outs = [((T, D), F32), ((T, D), BF), ((T, FF), BF), ((T, D), BF), ((S, D), BF), ((8, D), F32), ((1, FF), F32)]
    return pl.pallas_call(bwd_kernel, out_shape=[Z(*s) for s in outs],
        in_specs=[sm, vm, vm, vm] + [hbm] * 8, out_specs=[hbm] * 5 + [vm] * 2,
        scratch_shapes=[V((D, D), BF), V((D, 3840), BF), V((FF, D), BF), V((S, D), BF), V((S, 256), BF), V((8, S), F32), V((T, D), F32), V((T, FF), BF),
            V((T, D), BF), V((T, FF), BF), V((T, D), BF), V((T, D), F32), V((4, T, 256), BF), V((S, 256), BF),
            V((256, S), BF), V((256, S), BF), V((256, S), BF), V((256, S), F32), V((8, S), F32), V((S, 512), F32), V((S, D), BF),
            V((2, T, D), BF), V((3, T, D), BF), V((T, D), BF), V((T, D), F32),
            pltpu.SemaphoreType.DMA((8,)), pltpu.SemaphoreType.DMA((8,)), pltpu.SemaphoreType.DMA((13,)), pltpu.SemaphoreType.DMA((13,))],
        compiler_params=pltpu.CompilerParams(collective_id=cid, has_side_effects=True, vmem_limit_bytes=VMEM_LIMIT))(lim, g, x, vec, wq, wou, wd, qkv, o, lse, r, gp)

def place():
    d = lax.axis_index("dp"); f = lax.axis_index("fsdp")
    return d, f, d // 2, d % 2, f // 2, f % 2

def gather_kernel(nz, q4, ou, dn, wq, wou, we, wd, rq, rou, blk, blkq, local, ssem, rsem):
    d, f, z, y, x, c = place()
    q = z * 4 + y * 2 + x
    up, down = (d + 2, f), (d - 2, f)
    yp, xp, sp = (d ^ 1, f), (d, f ^ 2), (d, f ^ 1)
    bar = pltpu.get_barrier_semaphore()
    for dev in (sp, xp, (d, f ^ 3), yp):
        pl.semaphore_signal(bar, inc=1, device_id=dev, device_id_type=MESH)
    @pl.when(z > 0)
    def _(): pl.semaphore_signal(bar, inc=1, device_id=down, device_id_type=MESH)
    @pl.when(z < nz - 1)
    def _(): pl.semaphore_signal(bar, inc=1, device_id=up, device_id_type=MESH)
    pl.semaphore_wait(bar, 4 + (z > 0).astype(jnp.int32) + (z < nz - 1).astype(jnp.int32))

    sends = []
    def go(copy, pred=None):
        if pred is None:
            copy.start()
        else:
            pl.when(pred)(copy.start)
        sends.append((pred, copy))
    def got(region, sem, pred=None):
        w = remote(region, region, ssem.at[0], sem, sp)
        if pred is None: w.wait_recv()
        else: pl.when(pred)(w.wait_recv)

    n = [0]
    def sem():
        n[0] += 1
        return ssem.at[n[0] - 1], rsem.at[n[0] - 1]
    s_ou = sem(); go(remote(ou, rou, *s_ou, sp))
    s_q = [sem() for _ in range(4)]
    for k in range(1, 4):
        dst = f ^ k
        go(remote(q4.at[dst], rq.at[f], s_q[k][0], rsem.at[n[0] - 4 + k], (d, dst)))
    own_dn = wd.at[pl.ds(pl.multiple_of((q * 2 + c) * 96, 16), 96), :]
    s_dn = sem(); go(remote(dn, own_dn, *s_dn, sp))
    loc = [pltpu.make_async_copy(dn, own_dn, local.at[0])]
    loc[0].start()
    rq[f] = q4[f]
    got(rou, s_ou[1])
    mine, other = ou[...].astype(F32), rou[...].astype(F32)
    blk[...] = jnp.concatenate([jnp.where(c == 0, mine, other), jnp.where(c == 0, other, mine)], axis=0).astype(BF)
    row = pl.ds(pl.multiple_of(q * 48, 16), 48)
    l1 = pltpu.make_async_copy(blk.at[:, pl.ds(0, 3840)], wou.at[row, :], local.at[1]); l1.start()
    l2 = pltpu.make_async_copy(blk.at[:, pl.ds(3840, 128)], we.at[row, :], local.at[2]); l2.start()
    for k in range(1, 4):
        got(rq.at[f ^ k], s_q[k][1])
    blkq[...] = jnp.concatenate([rq[k].astype(F32) for k in range(4)], axis=0).astype(BF)
    l3 = pltpu.make_async_copy(blkq, wq.at[pl.ds(pl.multiple_of(d * 96, 16), 96), :], local.at[3]); l3.start()
    l2.wait(); l3.wait(); l1.wait(); loc[0].wait()
    other_dn = wd.at[pl.ds(pl.multiple_of((q * 2 + 1 - c) * 96, 16), 96), :]
    got(other_dn, s_dn[1])

    c1 = pl.multiple_of(c * 1920, 128)
    NA = 1280
    parts = {
        "Q": dict(ref=wq, rows=96, col0=0, cols=768, order="zy", sib=False),
        "E": dict(ref=we, rows=48, col0=0, cols=128, order="xyz", sib=False),
        "O": dict(ref=wou, rows=48, col0=c1, cols=NA, order="zxy", sib=True),
        "D": dict(ref=wd, rows=192, col0=pl.multiple_of(c * 384, 128), cols=384, order="zyx", sib=True),
        "P": dict(ref=wou, rows=48, col0=pl.multiple_of(c1 + NA, 128), cols=1920 - NA, order="xyz", sib=True),
    }
    def reg(p, r0, cnt):
        p = parts[p]
        return p["ref"].at[pl.ds(pl.multiple_of(r0 * p["rows"], 16), cnt * p["rows"]), pl.ds(p["col0"], p["cols"])]
    def push(p, r0, cnt, dev, pred=None):
        s, r = sem()
        region = reg(p, r0, cnt)
        go(remote(region, region, s, r, dev), pred)
        return r
    def recv(p, r0, cnt, r, pred=None, sib=True):
        got(reg(p, r0, cnt), r, pred)
        if sib and parts[p]["sib"]:
            rs = push(p, r0, cnt, sp, pred)
            late.append((p, r0, cnt, rs, pred))
    late = []
    slots = [(0, 0)] + [(s, k) for s in range(1, nz) for k in (0, 1)]
    def slot_z(s, k):
        return z - s if k == 0 else z + s
    def slot_ok(s, k):
        if s == 0: return None
        return (z - s >= 0) if k == 0 else (z + s < nz)
    def both(a, b):
        if a is None: return b
        return a & b
    zr = {}
    def zblock(p, zz):
        o = parts[p]["order"]
        if o == "zy": return zz * 2 + y, 1
        if o[0] == "z": return zz * 4 + y * 2 + x, 1
        return zz * 4, 4
    def zsend(p, s):
        for k in (0, 1):
            okc = slot_ok(s - 1, k) if s > 1 else None
            edge = (z < nz - 1) if k == 0 else (z > 0)
            r0, cnt = zblock(p, slot_z(s - 1, k))
            zr[p, s, k] = push(p, r0, cnt, up if k == 0 else down, both(okc, edge))
    def zrecv(p, s, then):
        for k in (0, 1):
            r0, cnt = zblock(p, slot_z(s, k))
            recv(p, r0, cnt, zr[p, s, k], slot_ok(s, k))
            if then: then(p, s, k)
    second = {}; third = {}
    def step2(p, s, k):
        o = parts[p]["order"]; zz = slot_z(s, k)
        if o == "zy": second[p, s, k] = push(p, zz * 2 + y, 1, yp, slot_ok(s, k))
        elif o[1] == "x": second[p, s, k] = push(p, zz * 4 + y * 2 + x, 1, xp, slot_ok(s, k))
        else: second[p, s, k] = push(p, zz * 4 + y * 2 + x, 1, yp, slot_ok(s, k))
    def recv2(p, s, k):
        o = parts[p]["order"]; zz = slot_z(s, k); ok = slot_ok(s, k)
        if o == "zy":
            recv(p, zz * 2 + 1 - y, 1, second[p, s, k], ok)
        elif o[1] == "x":
            recv(p, zz * 4 + y * 2 + 1 - x, 1, second[p, s, k], ok)
            third[p, s, k] = [(zz * 4 + (1 - y) * 2, 2, push(p, zz * 4 + y * 2, 2, yp, ok))]
        else:
            recv(p, zz * 4 + (1 - y) * 2 + x, 1, second[p, s, k], ok)
            third[p, s, k] = [(zz * 4 + yy * 2 + 1 - x, 1, push(p, zz * 4 + yy * 2 + x, 1, xp, ok)) for yy in range(2)]
    def recv3(p, s, k):
        for r0, cnt, r in third[p, s, k]:
            recv(p, r0, cnt, r, slot_ok(s, k))
    zp = ("Q", "O", "D")
    for p in zp: zsend(p, 1)
    e1 = push("E", q, 1, xp); p1 = push("P", q, 1, xp)
    for p in zp: step2(p, 0, 0)
    recv("E", z * 4 + y * 2 + 1 - x, 1, e1); e2 = push("E", z * 4 + y * 2, 2, yp)
    recv("P", z * 4 + y * 2 + 1 - x, 1, p1); p2 = push("P", z * 4 + y * 2, 2, yp)
    recv("E", z * 4 + (1 - y) * 2, 2, e2); zsend("E", 1)
    for p in zp:
        zrecv(p, 1, step2)
        if nz > 2: zsend(p, 2)
    recv("P", z * 4 + (1 - y) * 2, 2, p2); zsend("P", 1)
    for p in zp: recv2(p, 0, 0)
    zrecv("E", 1, None)
    if nz > 2: zsend("E", 2)
    for s in range(2, nz):
        for p in zp:
            zrecv(p, s, step2)
            if s + 1 < nz: zsend(p, s + 1)
        zrecv("E", s, None)
        if s + 1 < nz: zsend("E", s + 1)
        for p in zp:
            for k in (0, 1): recv2(p, s - 1, k)
        zrecv("P", s - 1, None)
        zsend("P", s)
        for p in zp[1:]:
            for k in ((0,) if s == 2 else (0, 1)): recv3(p, s - 2, k)
    for p in zp:
        for k in (0, 1): recv2(p, nz - 1, k)
    for s in ([nz - 2, nz - 1]):
        for p in zp[1:]:
            for k in (0, 1): recv3(p, s, k)
    zrecv("P", nz - 1, None)
    for p, r0, cnt, rs, pred in late:
        pp = parts[p]
        other = dict(pp); base = {"O": 0, "P": NA, "D": 0}[p]
        half = 384 if p == "D" else 1920
        col = pl.multiple_of((1 - c) * half + base, 128)
        region = pp["ref"].at[pl.ds(pl.multiple_of(r0 * pp["rows"], 16), cnt * pp["rows"]), pl.ds(col, pp["cols"])]
        got(region, rs, pred)
    for pred, copy in sends:
        if pred is None: copy.wait_send()
        else: pl.when(pred)(copy.wait_send)

NSEM = 400
def gather(q4, ou, dn, nz):
    hbm = pl.BlockSpec(memory_space=pltpu.HBM); vm = pl.BlockSpec(memory_space=pltpu.VMEM)
    S = jax.ShapeDtypeStruct
    return pl.pallas_call(partial(gather_kernel, nz),
        out_shape=(S((768, 768), BF), S((768, 3840), BF), S((768, 128), BF), S((3072, 768), BF)),
        in_specs=[vm] * 3, out_specs=[hbm] * 4,
        scratch_shapes=[pltpu.VMEM((4, 24, 768), BF), pltpu.VMEM((24, 3968), BF), pltpu.VMEM((48, 3968), BF), pltpu.VMEM((96, 768), BF),
            pltpu.SemaphoreType.DMA((4,)), pltpu.SemaphoreType.DMA((NSEM,)), pltpu.SemaphoreType.DMA((NSEM,))],
        compiler_params=pltpu.CompilerParams(collective_id=0, has_side_effects=True, vmem_limit_bytes=32 * 2**20))(q4, ou, dn)


def gather_any(q4, ou, dn):
    both = ("dp", "fsdp")
    mine = lax.dynamic_index_in_dim(lax.all_gather(q4, both, axis=0), lax.axis_index("fsdp"), 1, keepdims=False)
    full = lax.all_gather(ou, both, axis=0, tiled=True)
    return mine.reshape(D, D), full[:, :3840], full[:, 3840:], lax.all_gather(dn, both, axis=0, tiled=True)

def body(tokens, qkv_weight, out_weight, up_weight, down_weight, norm_gains, up_bias, pass_table, pass_index, lengths, cotangent):
    rd = qkv_weight.shape[0]
    q4 = jnp.pad(qkv_weight.reshape(rd, 3, 4, 192), ((0, 0), (0, 0), (0, 0), (0, 64))).transpose(2, 0, 1, 3).reshape(4, rd, D)
    chooser = [(jnp.arange(pass_table.shape[1], dtype=jnp.int32) == pass_index[n]).astype(F32) for n in range(2)]
    emb = jnp.stack([jnp.sum(pass_table.astype(F32) * ch[None, :], axis=1) for ch in chooser], axis=1).astype(BF)
    e = jnp.concatenate([norm_gains, emb, up_bias.reshape(rd, 4), jnp.zeros((rd, 120), BF)], axis=1)
    ou = jnp.concatenate([out_weight, up_weight, e], axis=1)
    if rd == 24:
        wq, wou, we, wd = gather(q4, ou, down_weight, lax.axis_size("dp") // 2)
    else:
        wq, wou, we, wd = gather_any(q4, ou, down_weight)
    vecs = we[:, 0:4].T.astype(F32)
    vec = [jnp.concatenate([vecs[0:2], vecs[2 + n:3 + n], jnp.zeros((5, D), F32)], axis=0) for n in range(2)]
    bias = we[:, 4:8].reshape(1, FF).astype(F32)
    row_pos = lax.axis_index("fsdp") * T + jnp.arange(T, dtype=jnp.int32)
    valid = (row_pos < lengths[0]).astype(F32)[:, None]
    xs = [tokens.astype(F32)]; kept = []
    for n in range(2):
        res = fwd(lengths, xs[n], vec[n], bias, wq, wou, wd, 1)
        xs.append(res[0]); kept.append(res[1:])
    block_out = (xs[2] * valid).astype(BF)
    g = cotangent.astype(F32) * valid
    grads = [None, None]; sums = [None, None]; bs = [None, None]
    for n in (1, 0):
        n1, qkv, o, lse, og, r, n2, gp, a = kept[n]
        g, dm, du, da, dqkv, sums[n], bs[n] = bwd(lengths, g, xs[n], vec[n], wq, wou, wd, qkv, o, lse, r, gp, 2)
        grads[n] = (a, dm, n2, du, og, da, n1, dqkv)
    tn = lambda a, b: lax.dot_general(a, b, (((0,), (0,)), ((), ())), preferred_element_type=F32)
    cat = lambda i, sh: jnp.concatenate([grads[0][i].reshape(sh), grads[1][i].reshape(sh)], axis=0)
    a, dm, n2, du = cat(0, (T, FF)), cat(1, (T, D)), cat(2, (T, D)), cat(3, (T, FF))
    og = jnp.concatenate([grads[n][4][:, :, :192].transpose(1, 0, 2).reshape(T, D) for n in range(2)], axis=0)
    da, n1, dqkv = cat(5, (T, D)), cat(6, (S, D)), cat(7, (S, D))
    down_grad = tn(a, dm); up_grad = tn(n2, du); out_grad = tn(og, da); qg = tn(n1, dqkv)
    ps = lambda v: lax.psum_scatter(v, ("dp", "fsdp"), scatter_dimension=0, tiled=True)
    f = lax.axis_index("fsdp")
    qg = qg.reshape(D, 3, 256)[:, :, :192]
    full = lax.dynamic_update_slice(jnp.zeros((D, 3, D), F32), qg, (0, 0, f * 192)).reshape(D, 3 * D)
    tot = lax.psum((sums[0], sums[1], bs[0] + bs[1]), ("dp", "fsdp"))
    idx = lax.axis_index("dp") * 4 + f
    own = lambda v: lax.dynamic_slice_in_dim(v, idx * rd, rd, 0)
    gains = own(jnp.stack([tot[0][0] + tot[1][0], tot[0][1] + tot[1][1]], axis=1))
    table = own(tot[0][2])[:, None] * chooser[0][None] + own(tot[1][2])[:, None] * chooser[1][None]
    bias_grad = lax.dynamic_slice_in_dim(tot[2][0], idx * rd * 4, rd * 4, 0)
    return (block_out, g, ps(full), ps(out_grad), ps(up_grad), ps(down_grad), gains, bias_grad, table)

def solution(mesh):
    a = P(("dp", "fsdp"), None); b = P(("dp", "fsdp"))
    return jax.shard_map(body, mesh=mesh, in_specs=(a, a, a, a, a, a, b, a, P(), P("dp"), a), out_specs=(a, a, a, a, a, a, a, b, a), check_vma=False)
```

time: 1270 us -> 835 us (0.66)
  Pallas kernels: 0 us -> 277 us
  matrix products: 236 us -> 29.4 us
  local copies, waits for them, and re-layouts: 196 us -> 36.8 us
  waiting for transfers between devices: 565 us -> 420 us
  blocking collectives: 156 us -> 39.8 us
  other arithmetic: 63.4 us -> 6.7 us
  loops' own time: 25.9 us -> 0 us
    pallas_call x0 -> x5, Pallas kernels: none -> 277 us  [the longest x2 117 us: bwd(): pl.pallas_call(bwd_kernel, out_shape=[Z(*s) for s in outs], in_specs=[sm,...]
    dot_general x136 -> x4, matrix products: 236 us -> 29.4 us  [body(): lax.dot_general(a, b, (((0,), (0,)), ((), ())), preferred_element_type=F32)]
    all_gather x6 -> x0, waiting for transfers between devices: 172 us -> none  [the longest x1 65.2 us: current_block(): lax.all_gather(up_weight, ('dp', 'fsdp'), axis=0, tiled=True)]
    unnamed x14 -> x5, waiting for transfers between devices: 8.34 us -> 125 us
    dynamic_slice x132 -> x1, local copies, waits for them, and re-layouts: 108 us -> 0.58 us  [body(): bias_grad = lax.dynamic_slice_in_dim(tot[2][0], idx * rd * 4, rd * 4, 0)]
    reduce_scatter x4 -> x3, waiting for transfers between devices: 384 us -> 294 us  [body(): lax.psum_scatter(v, ('dp', 'fsdp'), scatter_dimension=0, tiled=True)]
    all_gather x2 -> x0, blocking collectives: 80.4 us -> none  [the longest x1 43.7 us: current_block(): lax.all_gather(pass_table, ('dp', 'fsdp'), axis=0, tiled=True)]
    unnamed x2 -> x0, blocking collectives: 75.4 us -> none
  transfers between devices with their start and end apart: 12 -> 4, of which waited for: 8 -> 4; matrix products, arithmetic and copies ran while one was open for 17% -> 5% of each run, Pallas kernels for 0% -> 0%
where the time goes in v1:
time: 835 us; the launch traced here: 825 us
  waiting for transfers between devices  420 us (50%)
  Pallas kernels  277 us (33%)
  blocking collectives  39.8 us (5%)
  local copies, waits for them, and re-layouts  36.8 us (4%)
  matrix products  29.4 us (4%)
  between operations  15.2 us (2%)
    reduce_scatter x3, waiting for transfers between devices, body(): lax.psum_scatter(v, ('dp', 'fsdp'), scatter_dimension=0, tiled=True)  294 us
    unnamed x5, waiting for transfers between devices  125 us
    pallas_call x2, Pallas kernels, bwd(): pl.pallas_call(bwd_kernel, out_shape=[Z(*s) for s in outs], in_specs=[sm,...  117 us
    pallas_call x2, Pallas kernels, fwd(): pl.pallas_call(fwd_kernel, out_shape=[Z(*s) for s in outs], in_specs=[sm,...  91.6 us
    pallas_call x1, Pallas kernels, gather(): pl.pallas_call(partial(gather_kernel, nz), out_shape=(S((768, 768), BF),...  68.5 us
    psum x1, blocking collectives, body(): tot = lax.psum((sums[0], sums[1], bs[0] + bs[1]), ('dp', 'fsdp'))  39.8 us
    dot_general x4, matrix products, body(): lax.dot_general(a, b, (((0,), (0,)), ((), ())), preferred_element_type=F32)  29.4 us
    unnamed x43, local copies, waits for them, and re-layouts  22.1 us
  transfers between devices with their start and end apart: 4, of which 4 were waited for; matrix products, arithmetic and copies ran while one was open for 5% of the time, Pallas kernels for 0%

profile of v1, /device:TPU:1, one launch (start us, length us, event | category | flops | bytes accessed | tf_op | source)
XLA Modules:
  0.0 825.4 jit_solution(2284445392441218248)
XLA Ops:
  9.5 1.3 fusion.41
  15.8 68.5 %shard_map.178 = (bf16[768,768]{1,0:T(8,128)(2,1)S(1)}, bf16[768,3840]{1,0:T(8,128)(2,1)S(1)}, bf16[768,128]{1,0:T(8,128)(2,1)S(1)}, bf16[3072,768]{1,0:T(8,128)(2,1)S(1)}) custom-call(bf16[4,24,768]{2,1,0:T(8,128)(2,1)S(1)} %reshape.120.q4, bf16[24,3968]{1,0:T(8,128)(2,1)S(1)} %concatenate.34.ou, bf16[96,768]{1,0:T(8,128)(2,1)S(1)} %copy-done.3), custom_call_target="tpu_custom_call" | custom-call | tf_op jit(solution)/shard_map/pallas_call | solution.py:503
  84.3 2.5 copy-done
  86.8 2.2 copy-done.1
  94.4 43.7 %shard_map.179 = (f32[384,768]{1,0:T(8,128)}, bf16[4,384,768]{2,1,0:T(8,128)(2,1)}, bf16[1536,768]{1,0:T(8,128)(2,1)}, bf16[1536,256]{1,0:T(8,128)(2,1)}, f32[8,...) custom-call(s32[1]{0:T(128)} %copy.46.lim, ...), custom_call_target="tpu_custom_call" | custom-call | tf_op jit(solution)/shard_map/pallas_call | solution.py:206
  138.1 47.9 %shard_map.180 = (f32[384,768]{1,0:T(8,128)}, bf16[4,384,768]{2,1,0:T(8,128)(2,1)}, bf16[1536,768]{1,0:T(8,128)(2,1)}, bf16[1536,256]{1,0:T(8,128)(2,1)}, f32[8,...) custom-call(s32[1]{0:T(128)} %copy.46.lim, ...), custom_call_target="tpu_custom_call" | custom-call | tf_op jit(solution)/shard_map/pallas_call | solution.py:206
  189.0 1.4 convert_multiply_fusion
  190.4 59.1 %shard_map.181 = (f32[384,768]{1,0:T(8,128)}, bf16[384,768]{1,0:T(8,128)(2,1)}, bf16[384,3072]{1,0:T(8,128)(2,1)}, bf16[384,768]{1,0:T(8,128)(2,1)}, bf16[1536,7...) custom-call(s32[1]{0:T(128)} %copy.46.lim, f32[384,768]{1,0:T(8,128)} %get-tuple-element.112.g, ...), custom_call_target="tpu_custom_call" | custom-call | tf_op jit(solution)/shard_map/pallas_call | solution.py:321
  249.5 57.7 %shard_map.182 = (f32[384,768]{1,0:T(8,128)}, bf16[384,768]{1,0:T(8,128)(2,1)}, bf16[384,3072]{1,0:T(8,128)(2,1)}, bf16[384,768]{1,0:T(8,128)(2,1)}, bf16[1536,7...) custom-call(s32[1]{0:T(128)} %copy.46.lim, f32[384,768]{1,0:T(8,128)} %get-tuple-element.58.g, ...), custom_call_target="tpu_custom_call" | custom-call | tf_op jit(solution)/shard_map/pallas_call | solution.py:321
  307.3 3.6 fusion.15
  311.2 1.3 copy-done.15
  312.5 7.0 fusion
  319.5 3.4 broadcast_in_dim.5
  322.9 1.4 slice_dynamic-update-slice_fusion
  324.3 8.2 copy.42
  332.5 1.6 copy-done.16
  334.3 9.5 %fusion.7 = f32[768,3072]{1,0:T(8,128)} fusion(bf16[384,3072]{1,0:T(8,128)(2,1)S(1)} %copy-done.16, bf16[384,3072]{1,0:T(8,128)(2,1)} %get-tuple-element.75, bf16[384,768]{1,0:T(8,128)(2,1)} %get-tuple-element.74, bf16[384,768]{1,0:T(8,128)(2,1)S(1)} %copy-done.17), kind=kOutput, calls=%fused_computation.7 | convolution fusion | flops 3635675136 | bytes 15335424 | tf_op jit(solution)/shard_map/dot_general | solution.py:544
  344.1 1.3 copy-done.14
  345.6 9.4 %fusion.11 = f32[3072,768]{1,0:T(8,128)} fusion(bf16[384,3072]{1,0:T(8,128)(2,1)} %get-tuple-element.78, bf16[384,3072]{1,0:T(8,128)(2,1)S(1)} %copy-done.14, bf16[384,768]{1,0:T(8,128)(2,1)S(1)} %copy-done.18, bf16[384,768]{1,0:T(8,128)(2,1)} %get-tuple-element.79), kind=kOutput, calls=%fused_computation.11 | convolution fusion | flops 3635675136 | bytes 15335424 | tf_op jit(solution)/shard_map/dot_general | solution.py:544
  355.7 39.8 %all-reduce.2 = (f32[8,768]{1,0:T(8,128)S(1)}, f32[8,768]{1,0:T(8,128)S(1)}, f32[1,3072]{1,0:T(1,128)S(1)}) all-reduce(f32[8,768]{1,0:T(8,128)S(1)} %copy-done.10, f32[8,768]{1,0:T(8,128)S(1)} %copy-done.11, f32[1,3072]{1,0:T(1,128)S(1)} %add.83), channel_id=1, replica_groups=mesh['dp'=8,'fsdp'=4] {'dp','fsdp'}, use_global_device_ids=true, to_apply=%region_7.8 | all-reduce | flops 15360 | bytes 122880 | tf_op jit(solution)/shard_map/psum | solution.py:554
  397.6 11.5 %reduce-scatter.7.cloned.1.call-done = f32[24,768]{1,0:T(8,128)} async-done(((f32[768,768]{1,0:T(8,128)}), f32[24,768]{1,0:T(8,128)}) %reduce-scatter.7.cloned.1.call-update) | async-done | bytes 73744 | tf_op jit(solution)/shard_map/reduce_scatter | solution.py:550
  409.1 125.4 %reduce-scatter.13.cloned.1.call-done = f32[24,2304]{1,0:T(8,128)} async-done(((f32[768,2304]{1,0:T(8,128)}), f32[24,2304]{1,0:T(8,128)}) %reduce-scatter.13.cloned.1.call-update) | async-done | bytes 221200
  534.4 141.1 %reduce-scatter.9.cloned.1.call-done = f32[24,3072]{1,0:T(8,128)} async-done(((f32[768,3072]{1,0:T(8,128)}), f32[24,3072]{1,0:T(8,128)}) %reduce-scatter.9.cloned.1.call-update) | async-done | bytes 294928 | tf_op jit(solution)/shard_map/reduce_scatter | solution.py:550
  675.5 141.8 %reduce-scatter.11.cloned.1.call-done = f32[96,768]{1,0:T(8,128)} async-done(((f32[3072,768]{1,0:T(8,128)}), f32[96,768]{1,0:T(8,128)}) %reduce-scatter.11.cloned.1.call-update) | async-done | bytes 294928 | tf_op jit(solution)/shard_map/reduce_scatter | solution.py:550
  (79 shorter events, 19.6 us)
Async XLA Ops:
  7.2 83.9 %copy-start.7 = (bf16[384,768]{1,0:T(8,128)(2,1)S(1)}, bf16[384,768]{1,0:T(8,128)(2,1)}, u32[]{:S(2)}) copy-start(bf16[384,768]{1,0:T(8,128)(2,1)} %param.11) | copy-start | bytes 1769476
  7.2 401.9 %reduce-scatter.7.cloned.1.call-start = ((), (), s32[]{:S(2)}) async-start(), calls=%async_computation.4 | async-start | bytes 2433024 | tf_op jit(solution)/shard_map/reduce_scatter | solution.py:550
  14.9 0.9 copy-start.3
  84.2 2.5 copy-start
  86.8 2.2 copy-start.1
  89.0 1.1 copy-start.2
  186.0 2.4 copy-start.6
  187.3 1.5 copy-start.4
  187.3 1.6 copy-start.8
  249.5 57.8 %copy-start.9 = (bf16[384,4,192]{0,2,1:T(8,128)(2,1)S(1)}, bf16[384,4,192]{0,2,1:T(8,128)(2,1)}, u32[]{:S(2)}) copy-start(bf16[384,4,192]{0,2,1:T(8,128)(2,1)} %copy.40) | copy-start | bytes 1769476
  249.5 57.8 %copy-start.19 = (bf16[384,768]{1,0:T(8,128)(2,1)S(1)}, bf16[384,768]{1,0:T(8,128)(2,1)}, u32[]{:S(2)}) copy-start(bf16[384,768]{1,0:T(8,128)(2,1)} %get-tuple-element.72) | copy-start | bytes 1769476
  310.8 1.7 copy-start.15
  310.9 223.5 %reduce-scatter.13.cloned.1.call-start = ((), (), s32[]{:S(2)}) async-start(), calls=%async_computation.7 | async-start | bytes 7299072
  332.5 1.7 copy-start.16
  332.5 1.8 copy-start.17
  332.5 343.0 %reduce-scatter.9.cloned.1.call-start = ((), (), s32[]{:S(2)}) async-start(), calls=%async_computation.5 | async-start | bytes 9732096 | tf_op jit(solution)/shard_map/reduce_scatter | solution.py:550
  343.7 1.7 copy-start.14
  343.7 1.8 copy-start.18
  343.8 473.6 %reduce-scatter.11.cloned.1.call-start = ((), (), s32[]{:S(2)}) async-start(), calls=%async_computation.6 | async-start | bytes 9732096 | tf_op jit(solution)/shard_map/reduce_scatter | solution.py:550
  354.9 0.7 copy-start.12
  354.9 0.7 copy-start.13
  354.9 0.8 copy-start.10
  354.9 0.8 copy-start.11
  354.9 462.4 %copy-start.5 = (f32[384,768]{1,0:T(8,128)S(1)}, f32[384,768]{1,0:T(8,128)}, u32[]{:S(2)}) copy-start(f32[384,768]{1,0:T(8,128)} %get-tuple-element.128) | copy-start | bytes 3538948
Sparse Core Ops, SparseCore 0:
  311.0 98.0 reduce-scatter.6
  416.2 118.1 reduce-scatter.12
  540.9 134.5 reduce-scatter.8
  682.8 134.4 reduce-scatter.10

commit v2 on v1

--- a/solution.py
+++ b/solution.py
@@ -507,6 +507,286 @@
             pltpu.SemaphoreType.DMA((4,)), pltpu.SemaphoreType.DMA((NSEM,)), pltpu.SemaphoreType.DMA((NSEM,))],
         compiler_params=pltpu.CompilerParams(collective_id=0, has_side_effects=True, vmem_limit_bytes=32 * 2**20))(q4, ou, dn)
 
+def tn(left, right):
+    return lax.dot_general(left, right, (((0,), (0,)), ((), ())), preferred_element_type=F32)
+
+class Links:
+    def __init__(self, ssem, rsem, dev):
+        self.ssem, self.rsem, self.dev, self.n, self.sent = ssem, rsem, dev, 0, []
+    def sem(self):
+        self.n += 1
+        return self.n - 1
+    def send(self, src, dst, k, dev, pred=None):
+        copy = remote(src, dst, self.ssem.at[k], self.rsem.at[k], dev)
+        if pred is None: copy.start()
+        else: pl.when(pred)(copy.start)
+        self.sent.append((pred, copy))
+    def got(self, region, k, pred=None):
+        wait = remote(region, region, self.ssem.at[k], self.rsem.at[k], self.dev).wait_recv
+        if pred is None: wait()
+        else: pl.when(pred)(wait)
+    def close(self):
+        for pred, copy in self.sent:
+            if pred is None: copy.wait_send()
+            else: pl.when(pred)(copy.wait_send)
+
+def add_to(acc, inc):
+    acc[...] = (acc[...].astype(F32) + inc[...].astype(F32)).astype(BF)
+
+def line_sum(net, nz, z, up, down, block, recv):
+    sems = [[net.sem() for _ in range(nz)] for _ in range(2)]
+    for k in range(nz - 1):
+        for way, t, edge, behind, dev in ((0, nz - 1 - k, z < nz - 1 - k, z > 0, up), (1, k, z > k, z < nz - 1, down)):
+            inc = recv.at[way, t]
+            net.got(inc, sems[way][t], edge & behind)
+            pl.when(edge & behind)(lambda t=t, inc=inc: add_to(block(t), inc))
+            net.send(block(t), inc, sems[way][t], dev, edge)
+        yield
+    for t in range(nz):
+        if t > 0: net.got(recv.at[0, t], sems[0][t], z == t)
+        if t < nz - 1: net.got(recv.at[1, t], sems[1][t], z == t)
+
+def grads_kernel(nz, a_0, a_1, dm_0, dm_1, n2_0, n2_1, du_0, du_1, og_0, og_1, da_0, da_1, n1_0, n1_1, dq_0, dq_1, vin,
+                 down_o, outw_o, up_o, qkv_o, v_o,
+                 a, dm, n2, du, og, da, n1, dq, acc_d, stg_d, sib_d, acc_o, stg_o, sib_o, acc_p, stg_p, sib_p, acc_q,
+                 dx, dy, dz, oy, ox, oz, pz, py, px, qy, qz, qf, hop, half, vb, vr, lsem, ssem, rsem):
+    d, f, z, y, x, c = place()
+    up, down = (d + 2, f), (d - 2, f)
+    yp, xp, sp = (d ^ 1, f), (d, f ^ 2), (d, f ^ 1)
+    loads = []
+    def load(src, dst):
+        copy = pltpu.make_async_copy(src, dst, lsem.at[len(loads)])
+        copy.start(); loads.append(copy)
+    for src, dst, rows in ((a_0, a, T), (dm_0, dm, T), (n2_0, n2, T), (du_0, du, T), (da_0, da, T), (n1_0, n1, S), (dq_0, dq, S)):
+        other = {id(a_0): a_1, id(dm_0): dm_1, id(n2_0): n2_1, id(du_0): du_1, id(da_0): da_1, id(n1_0): n1_1, id(dq_0): dq_1}[id(src)]
+        load(src, dst.at[pl.ds(0, rows), :]); load(other, dst.at[pl.ds(rows, rows), :])
+    load(og_0, og.at[0]); load(og_1, og.at[1])
+    bar = pltpu.get_barrier_semaphore()
+    for dev in (sp, xp, (d, f ^ 3), yp):
+        pl.semaphore_signal(bar, inc=1, device_id=dev, device_id_type=MESH)
+    @pl.when(z > 0)
+    def _(): pl.semaphore_signal(bar, inc=1, device_id=down, device_id_type=MESH)
+    @pl.when(z < nz - 1)
+    def _(): pl.semaphore_signal(bar, inc=1, device_id=up, device_id_type=MESH)
+    pl.semaphore_wait(bar, 4 + (z > 0).astype(jnp.int32) + (z < nz - 1).astype(jnp.int32))
+    net = Links(ssem, rsem, sp)
+    turn = []
+    lo, hi = 0, nz - 1
+    while lo <= hi:
+        turn += [hi, lo] if lo < hi else [lo]
+        lo, hi = lo + 1, hi - 1
+    first = lambda v: jnp.where(c == 0, v[0], v[1])
+    second = lambda v: jnp.where(c == 0, v[1], v[0])
+
+    def vectors():
+        vb[...] = vin[...]
+        for i, dev in enumerate((sp, xp, yp)):
+            k = net.sem()
+            hop[i] = vb[...]
+            net.send(hop.at[i], vr.at[i], k, dev)
+            yield
+            net.got(vr.at[i], k)
+            vb[...] += vr[i]
+        for i in (3, 4): hop[i] = vb[...]
+        ks = [net.sem(), net.sem()]
+        for step in range(nz - 1):
+            yield
+            for way, pos, dev in ((0, z, up), (1, nz - 1 - z, down)):
+                @pl.when((pos == step) & (pos > 0))
+                def _(way=way):
+                    net.got(vr.at[3 + way], ks[way])
+                    hop[3 + way] += vr[3 + way]
+                net.send(hop.at[3 + way], vr.at[3 + way], ks[way], dev, pos == step)
+        for way, pos in ((0, z), (1, nz - 1 - z)):
+            net.got(vr.at[3 + way], ks[way], pos == nz - 1)
+        @pl.when(z > 0)
+        def _(): vb[...] += vr[3]
+        @pl.when(z < nz - 1)
+        def _(): vb[...] += vr[4]
+        v_o[...] = vb[...]
+
+    def down_part():
+        ks = {t: net.sem() for t in turn}
+        for t in turn:
+            g = tn(a[:, t * 768:(t + 1) * 768], dm[...]).reshape(4, 2, 96, D)
+            for q in range(4):
+                acc_d[t * 4 + q] = first(g[q]).astype(BF)
+                stg_d[t * 4 + q] = second(g[q]).astype(BF)
+            net.send(stg_d.at[pl.ds(t * 4, 4)], sib_d.at[pl.ds(t * 4, 4)], ks[t], sp)
+            yield
+        kx = {(t, j): net.sem() for t in turn for j in range(2)}
+        for t in turn:
+            net.got(sib_d.at[pl.ds(t * 4, 4)], ks[t])
+            add_to(acc_d.at[pl.ds(t * 4, 4)], sib_d.at[pl.ds(t * 4, 4)])
+            for j in range(2):
+                net.send(acc_d.at[t * 4 + j * 2 + 1 - x], dx.at[t * 2 + j], kx[t, j], xp)
+            yield
+        ky = {t: net.sem() for t in turn}
+        for t in turn:
+            for j in range(2):
+                net.got(dx.at[t * 2 + j], kx[t, j])
+                add_to(acc_d.at[t * 4 + j * 2 + x], dx.at[t * 2 + j])
+            net.send(acc_d.at[t * 4 + (1 - y) * 2 + x], dy.at[t], ky[t], yp)
+            yield
+        for t in turn:
+            net.got(dy.at[t], ky[t])
+            add_to(acc_d.at[t * 4 + y * 2 + x], dy.at[t])
+            if t != turn[-1]: yield
+        yield from line_sum(net, nz, z, up, down, lambda t: acc_d.at[t * 4 + y * 2 + x], dz)
+        down_o[...] = acc_d[z * 4 + y * 2 + x].astype(F32)
+        @pl.when(z > 0)
+        def _(): down_o[...] += dz[0, z].astype(F32)
+        @pl.when(z < nz - 1)
+        def _(): down_o[...] += dz[1, z].astype(F32)
+
+    def own_cols(ref, base, width, off, cols, mine):
+        cc = c if mine else 1 - c
+        return ref[:, pl.ds(pl.multiple_of(base + cc * width + off, 128), cols)]
+    def fill(dst, base, g):
+        n = g.shape[1]
+        dst[:, :, base:base + n] = g.astype(BF).reshape(16, 48, n)
+    def finish_cols(acc_block, incs, base, n):
+        total = acc_block.astype(F32)
+        for pred, inc in incs:
+            total = total + jnp.where(pred, inc.astype(F32), 0.0)
+        keep = jnp.where(c == 0, total[0:24], total[24:48])
+        give = jnp.where(c == 0, total[24:48], total[0:24])
+        half[0, :, base:base + n] = keep
+        half[1, :, base:base + n] = give
+
+    def wide_part():
+        for dst, mine in ((acc_p, True), (stg_p, False)):
+            fill(dst, 0, tn(n2[...], own_cols(du, 0, 1536, 896, 640, mine)))
+        kp = net.sem()
+        net.send(stg_p, sib_p, kp, sp)
+        yield
+        for dst, mine in ((acc_o, True), (stg_o, False)):
+            for j in range(4):
+                g = tn(og[0, j, :, 0:192], own_cols(da, 0, 384, 0, 384, mine)[0:T]) + tn(og[1, j, :, 0:192], own_cols(da, 0, 384, 0, 384, mine)[T:2 * T])
+                dst[j * 4:(j + 1) * 4, :, 0:384] = g.astype(BF).reshape(4, 48, 384)
+            fill(dst, 384, tn(n2[...], own_cols(du, 0, 1536, 0, 896, mine)))
+        ko = net.sem()
+        net.send(stg_o, sib_o, ko, sp)
+        net.got(sib_p, kp)
+        add_to(acc_p, sib_p)
+        lines = line_sum(net, nz, z, up, down, lambda t: acc_p.at[pl.ds(t * 4, 4)], pz)
+        next(lines)
+        yield
+        net.got(sib_o, ko)
+        ky = {t: net.sem() for t in turn}
+        for t in turn:
+            add_to(acc_o.at[pl.ds(t * 4, 4)], sib_o.at[pl.ds(t * 4, 4)])
+            net.send(acc_o.at[pl.ds(t * 4 + (1 - y) * 2, 2)], oy.at[pl.ds(t * 2, 2)], ky[t], yp)
+        yield
+        next(lines)
+        kx = {t: net.sem() for t in turn}
+        for t in turn:
+            net.got(oy.at[pl.ds(t * 2, 2)], ky[t])
+            add_to(acc_o.at[pl.ds(t * 4 + y * 2, 2)], oy.at[pl.ds(t * 2, 2)])
+            net.send(acc_o.at[t * 4 + y * 2 + 1 - x], ox.at[t], kx[t], xp)
+            yield
+        for _ in lines: yield
+        own = acc_p.at[pl.ds(z * 4, 4)]
+        @pl.when(z > 0)
+        def _(): add_to(own, pz.at[0, z])
+        @pl.when(z < nz - 1)
+        def _(): add_to(own, pz.at[1, z])
+        k1 = net.sem()
+        net.send(acc_p.at[pl.ds(z * 4 + (1 - y) * 2, 2)], py, k1, yp)
+        yield
+        for t in turn:
+            net.got(ox.at[t], kx[t])
+            add_to(acc_o.at[t * 4 + y * 2 + x], ox.at[t])
+        lines = line_sum(net, nz, z, up, down, lambda t: acc_o.at[t * 4 + y * 2 + x], oz)
+        next(lines)
+        yield
+        net.got(py, k1)
+        add_to(acc_p.at[pl.ds(z * 4 + y * 2, 2)], py)
+        k2 = net.sem()
+        net.send(acc_p.at[z * 4 + y * 2 + 1 - x], px, k2, xp)
+        yield
+        for _ in lines: yield
+        net.got(px, k2)
+        q = z * 4 + y * 2 + x
+        finish_cols(acc_p[q], [(True, px[...])], 1280, 640)
+        finish_cols(acc_o[q], [(z > 0, oz[0, z]), (z < nz - 1, oz[1, z])], 0, 1280)
+        k3 = net.sem()
+        net.send(half.at[1], half.at[2], k3, sp)
+        yield
+        net.got(half.at[2], k3)
+        for cc, s in ((c, 0), (1 - c, 2)):
+            outw_o[:, pl.ds(pl.multiple_of(cc * 384, 128), 384)] = half[s, :, 0:384]
+            up_o[:, pl.ds(pl.multiple_of(cc * 1536, 128), 1536)] = half[s, :, 384:1920]
+
+    def qkv_part():
+        ky = {t: net.sem() for t in turn}
+        for j in range(2):
+            g = tn(n1[:, j * 384:(j + 1) * 384], dq[...])
+            acc_q[j * 4:(j + 1) * 4] = g.astype(BF).reshape(4, 96, D)
+        for t in turn:
+            net.send(acc_q.at[t * 2 + 1 - y], qy.at[t], ky[t], yp)
+        yield
+        for t in turn:
+            net.got(qy.at[t], ky[t])
+            add_to(acc_q.at[t * 2 + y], qy.at[t])
+        yield from line_sum(net, nz, z, up, down, lambda t: acc_q.at[t * 2 + y], qz)
+        total = acc_q[z * 2 + y].astype(F32)
+        total = total + jnp.where(z > 0, qz[0, z].astype(F32), 0.0) + jnp.where(z < nz - 1, qz[1, z].astype(F32), 0.0)
+        for j in range(4): qf[0, j] = total[j * 24:(j + 1) * 24]
+        ks = [net.sem() for _ in range(4)]
+        for k in (1, 2, 3):
+            net.send(qf.at[0, f ^ k], qf.at[1, f], ks[k], (d, f ^ k))
+        qkv_o[f] = qf[0, f]
+        yield
+        for k in (1, 2, 3):
+            net.got(qf.at[1, f ^ k], ks[k])
+            qkv_o[f ^ k] = qf[1, f ^ k]
+
+    def need(*which):
+        for i in which: loads[i].wait()
+    need(0, 1, 2, 3)
+    dp_, wp, qp, vp = down_part(), wide_part(), qkv_part(), vectors()
+    alive = []
+    def turn_of(g):
+        try:
+            next(g)
+        except StopIteration:
+            alive.remove(g)
+    alive += [dp_, vp]
+    for _ in turn: turn_of(dp_)
+    turn_of(vp)
+    need(4, 5, 6, 7, 8, 9, 14, 15)
+    alive.append(wp)
+    turn_of(wp)
+    turn_of(dp_); turn_of(vp); turn_of(dp_)
+    turn_of(wp)
+    turn_of(dp_); turn_of(dp_)
+    need(10, 11, 12, 13)
+    alive.append(qp)
+    turn_of(wp)
+    turn_of(qp)
+    while alive:
+        for g in list(alive): turn_of(g)
+    net.close()
+
+def grads_sum(kept0, kept1, vin, nz):
+    Z = jax.ShapeDtypeStruct
+    hbm = pl.BlockSpec(memory_space=pltpu.HBM); vm = pl.BlockSpec(memory_space=pltpu.VMEM)
+    V = pltpu.VMEM
+    q = nz * 4
+    ins = []
+    for u, v in zip(kept0, kept1): ins += [u, v]
+    outs = [((96, D), F32), ((24, D), F32), ((24, FF), F32), ((4, 24, D), F32), ((8, D), F32)]
+    three = lambda *s: [V(s, BF)] * 3
+    return pl.pallas_call(partial(grads_kernel, nz), out_shape=[Z(*s) for s in outs],
+        in_specs=[hbm] * 16 + [vm], out_specs=[vm] * 5,
+        scratch_shapes=[V((2 * T, FF), BF), V((2 * T, D), BF), V((2 * T, D), BF), V((2 * T, FF), BF), V((2, 4, T, 256), BF), V((2 * T, D), BF), V((2 * S, D), BF), V((2 * S, D), BF)]
+            + three(q, 96, D) + three(q, 48, 1280) + three(q, 48, 640) + [V((2 * nz, 96, D), BF)]
+            + [V((2 * nz, 96, D), BF), V((nz, 96, D), BF), V((2, nz, 96, D), BF), V((2 * nz, 48, 1280), BF), V((nz, 48, 1280), BF), V((2, nz, 48, 1280), BF),
+               V((2, nz, 4, 48, 640), BF), V((2, 48, 640), BF), V((48, 640), BF), V((nz, 96, D), BF), V((2, nz, 96, D), BF), V((2, 4, 24, D), F32),
+               V((5, 8, D), F32), V((3, 24, 1920), F32), V((8, D), F32), V((5, 8, D), F32),
+               pltpu.SemaphoreType.DMA((16,)), pltpu.SemaphoreType.DMA((96,)), pltpu.SemaphoreType.DMA((96,))],
+        compiler_params=pltpu.CompilerParams(collective_id=3, has_side_effects=True, vmem_limit_bytes=VMEM_LIMIT))(*ins, vin)
 
 def gather_any(q4, ou, dn):
     both = ("dp", "fsdp")
@@ -541,23 +821,30 @@
         n1, qkv, o, lse, og, r, n2, gp, a = kept[n]
         g, dm, du, da, dqkv, sums[n], bs[n] = bwd(lengths, g, xs[n], vec[n], wq, wou, wd, qkv, o, lse, r, gp, 2)
         grads[n] = (a, dm, n2, du, og, da, n1, dqkv)
-    tn = lambda a, b: lax.dot_general(a, b, (((0,), (0,)), ((), ())), preferred_element_type=F32)
-    cat = lambda i, sh: jnp.concatenate([grads[0][i].reshape(sh), grads[1][i].reshape(sh)], axis=0)
-    a, dm, n2, du = cat(0, (T, FF)), cat(1, (T, D)), cat(2, (T, D)), cat(3, (T, FF))
-    og = jnp.concatenate([grads[n][4][:, :, :192].transpose(1, 0, 2).reshape(T, D) for n in range(2)], axis=0)
-    da, n1, dqkv = cat(5, (T, D)), cat(6, (S, D)), cat(7, (S, D))
-    down_grad = tn(a, dm); up_grad = tn(n2, du); out_grad = tn(og, da); qg = tn(n1, dqkv)
-    ps = lambda v: lax.psum_scatter(v, ("dp", "fsdp"), scatter_dimension=0, tiled=True)
+    flat = lambda n: [grads_of.reshape(S, D) if k == 6 else grads_of for k, grads_of in enumerate(grads[n])]
+    vin = jnp.concatenate([sums[0][0:2] + sums[1][0:2], sums[0][2:3], sums[1][2:3], (bs[0] + bs[1]).reshape(4, D)], axis=0)
     f = lax.axis_index("fsdp")
-    qg = qg.reshape(D, 3, 256)[:, :, :192]
-    full = lax.dynamic_update_slice(jnp.zeros((D, 3, D), F32), qg, (0, 0, f * 192)).reshape(D, 3 * D)
-    tot = lax.psum((sums[0], sums[1], bs[0] + bs[1]), ("dp", "fsdp"))
+    if rd == 24:
+        down_grad, out_grad, up_grad, q_grad, tot = grads_sum(flat(0), flat(1), vin, lax.axis_size("dp") // 2)
+    else:
+        down_grad, out_grad, up_grad, q_grad, tot = grads_any(flat(0), flat(1), vin, rd)
+    qkv_grad = q_grad.reshape(4, rd, 3, 256)[..., :192].transpose(1, 2, 0, 3).reshape(rd, 3 * D)
     idx = lax.axis_index("dp") * 4 + f
     own = lambda v: lax.dynamic_slice_in_dim(v, idx * rd, rd, 0)
-    gains = own(jnp.stack([tot[0][0] + tot[1][0], tot[0][1] + tot[1][1]], axis=1))
-    table = own(tot[0][2])[:, None] * chooser[0][None] + own(tot[1][2])[:, None] * chooser[1][None]
-    bias_grad = lax.dynamic_slice_in_dim(tot[2][0], idx * rd * 4, rd * 4, 0)
-    return (block_out, g, ps(full), ps(out_grad), ps(up_grad), ps(down_grad), gains, bias_grad, table)
+    gains = own(tot[0:2].T)
+    table = own(tot[2])[:, None] * chooser[0][None] + own(tot[3])[:, None] * chooser[1][None]
+    bias_grad = lax.dynamic_slice_in_dim(tot[4:8].reshape(FF), idx * rd * 4, rd * 4, 0)
+    return (block_out, g, qkv_grad, out_grad, up_grad, down_grad, gains, bias_grad, table)
+
+def grads_any(kept0, kept1, vin, rd):
+    both = ("dp", "fsdp")
+    a, dm, n2, du, og, da, n1, dq = [jnp.concatenate([u, v], axis=0) for u, v in zip(kept0, kept1)]
+    heads = og.reshape(2, 4, T, 256)[..., :192].transpose(0, 2, 1, 3).reshape(2 * T, D)
+    scatter = lambda v: lax.psum_scatter(v, both, scatter_dimension=0, tiled=True)
+    q = tn(n1, dq).reshape(-1, 4, rd, D)
+    place_q = lax.dynamic_update_slice(jnp.zeros((4,) + (D // rd, rd, D), F32), q.reshape(1, D // rd, rd, D), (lax.axis_index("fsdp"), 0, 0, 0))
+    q_grad = lax.psum_scatter(place_q, both, scatter_dimension=1, tiled=True).reshape(4, rd, D)
+    return scatter(tn(a, dm)), scatter(tn(heads, da)), scatter(tn(n2, du)), q_grad, lax.psum(vin, both)
 
 def solution(mesh):
     a = P(("dp", "fsdp"), None); b = P(("dp", "fsdp"))

time: 835 us -> 440 us (0.53)
  waiting for transfers between devices: 420 us -> 0 us
  Pallas kernels: 277 us -> 399 us
  blocking collectives: 39.8 us -> 0 us
  matrix products: 29.4 us -> 0 us
  local copies, waits for them, and re-layouts: 36.8 us -> 22.7 us
  between operations: 15.2 us -> 2.14 us
    reduce_scatter x3 -> x0, waiting for transfers between devices: 294 us -> none  [body(): lax.psum_scatter(v, ('dp', 'fsdp'), scatter_dimension=0, tiled=True)]
    unnamed x5 -> x0, waiting for transfers between devices: 125 us -> none
    pallas_call x0 -> x1, Pallas kernels: none -> 122 us  [grads_sum(): pl.pallas_call(partial(grads_kernel, nz), out_shape=[Z(*s) for s in outs]...]
    psum x1 -> x0, blocking collectives: 39.8 us -> none  [body(): tot = lax.psum((sums[0], sums[1], bs[0] + bs[1]), ('dp', 'fsdp'))]
    dot_general x4 -> x0, matrix products: 29.4 us -> none  [body(): lax.dot_general(a, b, (((0,), (0,)), ((), ())), preferred_element_type=F32)]
    unnamed x43 -> x31, local copies, waits for them, and re-layouts: 22.1 us -> 9.65 us
  transfers between devices with their start and end apart: 4 -> 0, of which waited for: 4 -> 0; matrix products, arithmetic and copies ran while one was open for 5% -> 0% of each run, Pallas kernels for 0% -> 0%
where the time goes in v2:
time: 440 us; the launch traced here: 433 us
  Pallas kernels  399 us (91%)
  local copies, waits for them, and re-layouts  22.7 us (5%)
  other arithmetic  9.43 us (2%)
    pallas_call x1, Pallas kernels, grads_sum(): pl.pallas_call(partial(grads_kernel, nz), out_shape=[Z(*s) for s in outs]...  122 us
    pallas_call x2, Pallas kernels, bwd(): pl.pallas_call(bwd_kernel, out_shape=[Z(*s) for s in outs], in_specs=[sm,...  117 us
    pallas_call x2, Pallas kernels, fwd(): pl.pallas_call(fwd_kernel, out_shape=[Z(*s) for s in outs], in_specs=[sm,...  91.8 us
    pallas_call x1, Pallas kernels, gather(): pl.pallas_call(partial(gather_kernel, nz), out_shape=(S((768, 768), BF),...  68.5 us
    unnamed x31, local copies, waits for them, and re-layouts  9.65 us

profile of v2, /device:TPU:1, one launch (start us, length us, event | category | flops | bytes accessed | tf_op | source)
XLA Modules:
  0.0 433.0 jit_solution(658417693679903876)
XLA Ops:
  1.5 1.3 fusion.6
  2.8 1.3 compare_convert_fusion
  4.1 0.8 fusion.1
  5.1 0.7 copy.32
  5.8 0.7 reshape.84
  6.6 1.1 reshape.82
  8.2 1.1 convert_element_type.48.x
  9.3 68.5 %shard_map.178 = (bf16[768,768]{1,0:T(8,128)(2,1)S(1)}, bf16[768,3840]{1,0:T(8,128)(2,1)S(1)}, bf16[768,128]{1,0:T(8,128)(2,1)S(1)}, bf16[3072,768]{1,0:T(8,128)(2,1)S(1)}) custom-call(bf16[4,24,768]{2,1,0:T(8,128)(2,1)S(1)} %reshape.83.q4, bf16[24,3968]{1,0:T(8,128)(2,1)S(1)} %concatenate.13.ou, bf16[96,768]{1,0:T(8,128)(2,1)S(1)} %copy-done.3), custom_call_target="tpu_custom_call" | custom-call | tf_op jit(solution)/shard_map/pallas_call | solution.py:503
  77.8 2.5 copy-done
  80.3 2.2 copy-done.1
  82.5 1.0 copy-done.2
  85.1 0.9 reshape.91.bias
  86.0 43.8 %shard_map.179 = (f32[384,768]{1,0:T(8,128)}, bf16[4,384,768]{2,1,0:T(8,128)(2,1)}, bf16[1536,768]{1,0:T(8,128)(2,1)}, bf16[1536,256]{1,0:T(8,128)(2,1)}, f32[8,...) custom-call(s32[1]{0:T(128)} %copy.41.lim, ...), custom_call_target="tpu_custom_call" | custom-call | tf_op jit(solution)/shard_map/pallas_call | solution.py:206
  129.8 48.0 %shard_map.180 = (f32[384,768]{1,0:T(8,128)}, bf16[4,384,768]{2,1,0:T(8,128)(2,1)}, bf16[1536,768]{1,0:T(8,128)(2,1)}, bf16[1536,256]{1,0:T(8,128)(2,1)}, f32[8,...) custom-call(s32[1]{0:T(128)} %copy.41.lim, ...), custom_call_target="tpu_custom_call" | custom-call | tf_op jit(solution)/shard_map/pallas_call | solution.py:206
  177.8 2.7 convert_multiply_fusion
  180.5 59.1 %shard_map.181 = (f32[384,768]{1,0:T(8,128)}, bf16[384,768]{1,0:T(8,128)(2,1)}, bf16[384,3072]{1,0:T(8,128)(2,1)}, bf16[384,768]{1,0:T(8,128)(2,1)}, bf16[1536,7...) custom-call(s32[1]{0:T(128)} %copy.41.lim, f32[384,768]{1,0:T(8,128)} %get-tuple-element.99.g, ...), custom_call_target="tpu_custom_call" | custom-call | tf_op jit(solution)/shard_map/pallas_call | solution.py:321
  239.6 57.7 %shard_map.182 = (f32[384,768]{1,0:T(8,128)}, bf16[384,768]{1,0:T(8,128)(2,1)}, bf16[384,3072]{1,0:T(8,128)(2,1)}, bf16[384,768]{1,0:T(8,128)(2,1)}, bf16[1536,7...) custom-call(s32[1]{0:T(128)} %copy.41.lim, f32[384,768]{1,0:T(8,128)} %get-tuple-element.63.g, ...), custom_call_target="tpu_custom_call" | custom-call | tf_op jit(solution)/shard_map/pallas_call | solution.py:321
  297.3 0.7 add_reduce_fusion
  298.8 0.8 slice_add_fusion
  301.0 121.7 %shard_map.183 = (f32[96,768]{1,0:T(8,128)}, f32[24,768]{1,0:T(8,128)}, f32[24,3072]{1,0:T(8,128)}, f32[4,24,768]{2,1,0:T(8,128)}, f32[8,768]{1,0:T(8,128)}) custom-call(bf16[384,3072]{1,0:T(8,128)(2,1)} %get-tuple-element.70.a_0, bf16[384,3072]{1,0:T(8,128)(2,1)} %get-tuple-element.71.a_1, bf16[384,768]{1,0:T(8,128)(2,1)} %get-tuple-element.72.dm_0, ...), custom_call_target="tpu_custom_call" | custom-call | tf_op jit(solution)/shard_map/pallas_call | solution.py:781
  424.0 0.8 fusion.5
  427.0 1.2 reshape.88
  428.5 0.9 reshape.89
  429.4 1.0 copy.42
  (57 shorter events, 10.3 us)
Async XLA Ops:
  0.6 7.4 %copy-start.9 = (bf16[24,3072]{1,0:T(8,128)(2,1)S(1)}, bf16[24,3072]{1,0:T(8,128)(2,1)}, u32[]{:S(2)}) copy-start(bf16[24,3072]{1,0:T(8,128)(2,1)} %param.14) | copy-start | bytes 442372
  0.7 7.4 %copy-start.11 = (bf16[24,768]{1,0:T(8,128)(2,1)S(1)}, bf16[24,768]{1,0:T(8,128)(2,1)}, u32[]{:S(2)}) copy-start(bf16[24,768]{1,0:T(8,128)(2,1)} %param.13) | copy-start | bytes 110596
  0.7 7.5 %copy-start.5 = (bf16[384,768]{1,0:T(8,128)(2,1)S(1)}, bf16[384,768]{1,0:T(8,128)(2,1)}, u32[]{:S(2)}) copy-start(bf16[384,768]{1,0:T(8,128)(2,1)} %param.11) | copy-start | bytes 1769476
  7.8 1.4 copy-start.3
  77.7 2.5 copy-start
  80.3 2.2 copy-start.1
  82.5 1.0 copy-start.2
  129.8 48.0 %copy-start.6 = (bf16[384,768]{1,0:T(8,128)(2,1)S(1)}, bf16[384,768]{1,0:T(8,128)(2,1)}, u32[]{:S(2)}) copy-start(bf16[384,768]{1,0:T(8,128)(2,1)} %param.21) | copy-start | bytes 1769476
  239.6 57.7 %copy-start.12 = (f32[1,3072]{1,0:T(1,128)S(1)}, f32[1,3072]{1,0:T(1,128)}, u32[]{:S(2)}) copy-start(f32[1,3072]{1,0:T(1,128)} %get-tuple-element.89) | copy-start | bytes 36868
  427.0 2.4 copy-start.4
  429.4 1.0 copy-start.10
  429.4 1.7 copy-start.8
  429.4 2.4 copy-start.7

commit v3 on v1

--- a/solution.py
+++ b/solution.py
@@ -9,7 +9,7 @@
 MESH = pl.DeviceIdType.MESH
 NEG = -1e30
 QB = 512
-VMEM_LIMIT = 58 * 2**20
+VMEM_LIMIT = 62 * 2**20
 
 def remote(src, dst, ssem, rsem, dev):
     return pltpu.make_async_remote_copy(src_ref=src, dst_ref=dst, send_sem=ssem, recv_sem=rsem, device_id=dev, device_id_type=MESH)
@@ -49,9 +49,14 @@
     parts.append(jnp.where(ok, sT[lo:], NEG))
     return parts[0] if len(parts) == 1 else jnp.concatenate(parts, 0)
 
+def half_mask(index, h):
+    edge = lax.full_like(index, 64)
+    return lax.lt(index, edge) if h % 2 == 0 else lax.ge(index, edge)
+
 def pick(xT, h):
     r = lax.broadcasted_iota(jnp.int32, xT.shape, 0)
-    return jnp.where((r // 64) == (h % 2), xT, jnp.zeros_like(xT))
+    mine = half_mask(r, h) if isinstance(h, int) else (r // 64) == (h % 2)
+    return jnp.where(mine, xT, jnp.zeros_like(xT))
 
 def slot_of(h, base=0):
     return pl.ds(pl.multiple_of(base + (h // 2) * 128, 128), 128)
@@ -71,24 +76,26 @@
         return 0
     lax.fori_loop(0, 3, head, 0)
 
-def bwd_block(i, qkv, do, lse, limit, qT, kT, doT, dqT, delta, dkv):
-    keys = (i + 1) * QB
-    cols = pl.ds(i * QB, QB)
-    def head(h, _):
-        hr = pl.ds(pl.multiple_of(h * 64, 64), 64)
-        lm = (lax.broadcasted_iota(jnp.int32, (QB, 128), 1) // 64) == (h % 2)
-        sT = dot(qkv[0:keys, slot_of(h, 256)], pick(qT[slot_of(h), cols], h))
-        sT = mask_scores(sT, i, limit)
-        p = jnp.exp(sT - lse[pl.ds(h, 1), cols])
-        dp = dot(qkv[0:keys, slot_of(h, 512)], pick(doT[slot_of(h), cols], h))
-        dsT = (p * (dp - delta[pl.ds(h, 1), cols])).astype(BF)
-        dqT[hr, cols] = dot(kT[hr, 0:keys], dsT)
-        qn = qkv[cols, slot_of(h)]
-        dn = do[cols, slot_of(h)]
-        dkv[0:keys, slot_of(h)] += dot(dsT, jnp.where(lm, qn, jnp.zeros_like(qn)))
-        dkv[0:keys, slot_of(h, 256)] += dot(p.astype(BF), jnp.where(lm, dn, jnp.zeros_like(dn)))
-        return 0
-    lax.fori_loop(0, 3, head, 0)
+def bwd_block(i, kc, h, qkv, do, lse, limit, qT, kT, doT, dqT, delta, dkv):
+    keys, cols = pl.ds(kc * QB, QB), pl.ds(i * QB, QB)
+    slot, hr = pl.ds((h // 2) * 128, 128), pl.ds(h * 64, 64)
+    after = lambda base: pl.ds(base + (h // 2) * 128, 128)
+    lane = lax.broadcasted_iota(jnp.int32, (QB, 128), 1)
+    lm = half_mask(lane, h)
+    sT = dot(qkv[keys, after(256)], pick(qT[slot, cols], h))
+    p = jnp.exp(sT - lse[h:h + 1, cols])
+    if kc == i or (kc + 1) * QB > 1024:
+        kpos = kc * QB + lax.broadcasted_iota(jnp.int32, (QB, QB), 0)
+        ok = kpos < limit
+        if kc == i: ok = ok & (kpos <= i * QB + lax.broadcasted_iota(jnp.int32, (QB, QB), 1))
+        p = jnp.where(ok, p, 0.0)
+    dp = dot(qkv[keys, after(512)], pick(doT[slot, cols], h))
+    dsT = (p * (dp - delta[h:h + 1, cols])).astype(BF)
+    step = dot(kT[hr, keys], dsT)
+    dqT[hr, cols] = step if kc == 0 else dqT[hr, cols] + step
+    qn, dn = qkv[cols, slot], do[cols, slot]
+    dkv[keys, slot] += dot(dsT, jnp.where(lm, qn, jnp.zeros_like(qn)))
+    dkv[keys, after(256)] += dot(p.astype(BF), jnp.where(lm, dn, jnp.zeros_like(dn)))
 
 def group_barrier(d, f):
     bar = pltpu.get_barrier_semaphore()
@@ -210,126 +217,488 @@
             pltpu.SemaphoreType.DMA((3,)), pltpu.SemaphoreType.DMA((16,)), pltpu.SemaphoreType.DMA((12,)), pltpu.SemaphoreType.DMA((12,))],
         compiler_params=pltpu.CompilerParams(collective_id=cid, has_side_effects=True, vmem_limit_bytes=VMEM_LIMIT))(lim, x, vec, bias, wq, wou, wd)
 
-def bwd_kernel(lim, g, x, vec, wq_h, wou_h, wd_h, qkv_h, o_h, lse_h, r_h, gp_h,
-               go_h, dm_h, du_h, da_h, dqkv_h, sums, bsum,
-               wq, wou, wd, qkv, o, lse, r, gp, dm, du, da, dr, dos, do, qT, kT, doT, dqT, delta, dkv, dqkv, mine, part, inc, go,
-               lsem, osem, ssem, rsem):
-    d = lax.axis_index("dp"); f = lax.axis_index("fsdp")
-    loads = [pltpu.make_async_copy(s, t, lsem.at[i]) for i, (s, t) in enumerate(
-        [(wd_h, wd), (gp_h, gp), (wou_h, wou), (r_h, r), (qkv_h, qkv), (o_h, o), (lse_h, lse), (wq_h, wq)])]
-    for c in loads: c.start()
-    group_barrier(d, f)
-    stores = []
-    def store(src, dst):
-        c = pltpu.make_async_copy(src, dst, osem.at[len(stores)])
-        c.start(); stores.append(c)
-    limit = lim[0]
-    g0, g1, emb = vec[0:1, :], vec[1:2, :], vec[2:3, :]
-    sends = []
-    def send(src, dst, k, dev):
-        c = remote(src, dst, ssem.at[k], rsem.at[k], dev)
-        c.start(); sends.append(c)
-    def got(region, k):
-        remote(region, region, ssem.at[k], rsem.at[k], (d, f ^ 1)).wait_recv()
-    dm[...] = g[...].astype(BF)
-    store(dm, dm_h)
-    loads[0].wait(); loads[1].wait()
-    W = 768
-    def up_tile(j, _):
-        cols = pl.ds(pl.multiple_of(j * W, 128), W)
-        t = (nt(dm[...], wd[cols, :]) * gp[:, cols].astype(F32)).astype(BF)
-        du[:, cols] = t
-        bsum[:, cols] = jnp.sum(t.astype(F32), axis=0, keepdims=True)
-        return 0
-    lax.fori_loop(0, FF // W, up_tile, 0)
-    store(du, du_h)
-    loads[2].wait(); loads[3].wait()
-    sums[...] = jnp.zeros_like(sums)
-    def norm2(j, _):
-        rows = rows_at(j * 128, 128)
-        e = nt(du[rows, :], wou[:, D:])
-        xhat, scale = normed(r[rows, :])
-        sums[1:2, :] += jnp.sum(e * xhat, axis=0, keepdims=True)
-        t = g[rows, :] + norm_back(xhat, scale, e, g1)
-        dr[rows, :] = t
-        da[rows, :] = t.astype(BF)
-        return 0
-    lax.fori_loop(0, T // 128, norm2, 0)
-    store(da, da_h)
-    for k in (3, 2, 1, 0):
-        b = f ^ k
-        dos[b, :, 0:192] = nt(da[...], wou[rows_at(b * 192, 192), 0:D]).astype(BF)
-        dos[b, :, 192:256] = jnp.zeros((T, 64), BF)
-        if k:
-            send(dos.at[b], do.at[rows_at(f * T, T), :], k, (d, b))
-        else:
-            do[rows_at(f * T, T), :] = dos[b]
-    for c in loads[4:]: c.wait()
-    qT[...] = (qkv[:, 0:256] * 0.125).astype(BF).T
-    kT[...] = qkv[:, 256:512].T
-    dqT[192:256, :] = jnp.zeros((64, S), F32)
-    dkv[...] = jnp.zeros_like(dkv)
-    for k in (1, 2, 3): got(do.at[rows_at((f ^ k) * T, T), :], k)
-    doT[...] = do[...].T
-    prod = (do[...].astype(F32) * o[...].astype(F32)).T
-    for h in range(3):
-        delta[h:h + 1, :] = jnp.sum(prod[h * 64:h * 64 + 64], axis=0, keepdims=True)
-    for i in range(S // QB):
-        bwd_block(i, qkv, do, lse, limit, qT, kT, doT, dqT, delta, dkv)
-    dqkv[:, 0:256] = (dqT[...] * 0.125).astype(BF).T
-    dqkv[:, 256:512] = (dkv[:, 0:256] * 0.125).astype(BF)
-    dqkv[:, 512:768] = dkv[:, 256:512].astype(BF)
-    store(dqkv, dqkv_h)
-    def partial_rows(b, j):
-        return nt(dqkv[rows_at(b * T + j * CH, CH), :], wq[...])
-    for j in range(3):
-        rows = pl.ds(j * CH, CH)
-        mine[0, rows, :] = partial_rows(f ^ 3, j).astype(BF)
-        send(mine.at[0, rows, :], part.at[0, rows, :], 4 + j, (d, f ^ 1))
-    for j in range(3):
-        rows = pl.ds(j * CH, CH)
-        t = partial_rows(f ^ 2, j)
-        got(part.at[0, rows, :], 4 + j)
-        inc[rows, :] = (t + part[0, rows, :].astype(F32)).astype(BF)
-        send(inc.at[rows, :], part.at[2, rows, :], 7 + j, (d, f ^ 2))
-    for j in range(3):
-        rows = pl.ds(j * CH, CH)
-        mine[1, rows, :] = partial_rows(f ^ 1, j).astype(BF)
-        send(mine.at[1, rows, :], part.at[1, rows, :], 10 + j, (d, f ^ 1))
-    for j in range(3):
-        rows = pl.ds(j * CH, CH)
-        go[rows, :] = partial_rows(f, j)
-    for j in range(3):
-        rows = pl.ds(j * CH, CH)
-        got(part.at[1, rows, :], 10 + j)
-        got(part.at[2, rows, :], 7 + j)
-        e = go[rows, :] + part[1, rows, :].astype(F32) + part[2, rows, :].astype(F32)
-        xhat, scale = normed(x[rows, :].astype(F32) + emb)
-        sums[0:1, :] += jnp.sum(e * xhat, axis=0, keepdims=True)
-        t = dr[rows, :] + norm_back(xhat, scale, e, g0)
-        sums[2:3, :] += jnp.sum(t, axis=0, keepdims=True)
-        go[rows, :] = t
-    store(go, go_h)
-    for c in sends: c.wait_send()
-    for c in stores: c.wait()
-
-def bwd(lim, g, x, vec, wq, wou, wd, qkv, o, lse, r, gp, cid):
-    Z = jax.ShapeDtypeStruct
-    hbm = pl.BlockSpec(memory_space=pltpu.HBM); vm = pl.BlockSpec(memory_space=pltpu.VMEM); sm = pl.BlockSpec(memory_space=pltpu.SMEM)
-    V = pltpu.VMEM
-    outs = [((T, D), F32), ((T, D), BF), ((T, FF), BF), ((T, D), BF), ((S, D), BF), ((8, D), F32), ((1, FF), F32)]
-    return pl.pallas_call(bwd_kernel, out_shape=[Z(*s) for s in outs],
-        in_specs=[sm, vm, vm, vm] + [hbm] * 8, out_specs=[hbm] * 5 + [vm] * 2,
-        scratch_shapes=[V((D, D), BF), V((D, 3840), BF), V((FF, D), BF), V((S, D), BF), V((S, 256), BF), V((8, S), F32), V((T, D), F32), V((T, FF), BF),
-            V((T, D), BF), V((T, FF), BF), V((T, D), BF), V((T, D), F32), V((4, T, 256), BF), V((S, 256), BF),
-            V((256, S), BF), V((256, S), BF), V((256, S), BF), V((256, S), F32), V((8, S), F32), V((S, 512), F32), V((S, D), BF),
-            V((2, T, D), BF), V((3, T, D), BF), V((T, D), BF), V((T, D), F32),
-            pltpu.SemaphoreType.DMA((8,)), pltpu.SemaphoreType.DMA((8,)), pltpu.SemaphoreType.DMA((13,)), pltpu.SemaphoreType.DMA((13,))],
-        compiler_params=pltpu.CompilerParams(collective_id=cid, has_side_effects=True, vmem_limit_bytes=VMEM_LIMIT))(lim, g, x, vec, wq, wou, wd, qkv, o, lse, r, gp)
+
+ZERO = [None]
+
+def at(ref, *index):
+    return ref.at[tuple(ZERO[0] + i if isinstance(i, int) else i for i in index)]
+
+def tn(left, right):
+    return lax.dot_general(left, right, (((0,), (0,)), ((), ())), preferred_element_type=F32)
+
+def when(pred, act):
+    if pred is None: act()
+    else: pl.when(pred)(act)
+
+class Links:
+    def __init__(self, ssem, rsem, dev):
+        self.ssem, self.rsem, self.dev, self.n, self.sent = ssem, rsem, dev, 0, []
+    def sem(self):
+        self.n += 1
+        return self.n - 1
+    def send(self, src, dst, k, dev, pred=None):
+        when(pred, remote(src, dst, at(self.ssem, k), at(self.rsem, k), dev).start)
+        self.sent.append((pred, src, k))
+    def got(self, region, k, pred=None):
+        when(pred, remote(region, region, at(self.ssem, k), at(self.rsem, k), self.dev).wait_recv)
+    def close(self):
+        for pred, src, k in self.sent:
+            base = getattr(src, "ref", src)
+            like = at(base, *([0] * (len(base.shape) - len(src.shape)) + [pl.ds(0, n) for n in src.shape]))
+            when(pred, remote(like, like, at(self.ssem, k), at(self.rsem, k), self.dev).wait_send)
+        self.sent = []
+
+PLAN = (
+    (), ("a3", "b3"), ("a0", "b0"), ("a2", "b2"), ("a3", "b3", "a1", "b1"), (), ("a0", "b0"), (), ("a3", "b3", "a2", "b2", "a1", "b1"),
+    ("a3", "a0", "b0", "b2"), ("a3", "b3", "a0", "b0", "a2", "b2", "b1", "p3", "p0", "p2", "p1", "o3", "o0", "o2", "o1", "a3", "b3", "a0", "a2", "a1"),
+    (), (), ("b0", "b2"), ("b1",), ("b3",), ("a0", "a2"), (), ("b0", "o3", "b1"), ("p3", "p0"), (), (), (), ("o3", "o0"), ("p2",), (), (),
+    ("p3", "p0"), ("o0", "o2"), ("p1",), ("a1",), ("p2",), (), ("o3", "o0", "o2", "o1", "p3"), ("p0",),
+    ("a1", "p1", "o3", "o2", "o1", "G", "q3", "q0", "q2", "q1", "o0", "pe"),
+    ("o3", "o2", "o1", "G", "q3", "q0", "r3", "r0", "r2", "r1", "o0", "G", "V", "q2"),
+    ("V", "q1", "q3", "q0", "o1", "V", "pe", "r3", "r0", "q3", "q0", "V", "pe", "r2", "q3", "q0", "r3", "r0", "r1", "q2", "r2", "q1", "V", "r3", "r0", "q2", "r1", "re", "q1", "V", "re", "V"),
+)
+
+class Agenda:
+    def __init__(self, plan): self.plan, self.jobs, self.point = plan, {}, 0
+    def add(self, name, job): self.jobs[name] = job
+    def step(self, name):
+        if next(self.jobs[name], self) is self: del self.jobs[name]
+    def run(self, hold=False):
+        names = self.plan[self.point] if self.point < len(self.plan) else ()
+        self.point += 1
+        for name in names: self.step(name)
+    def finish(self):
+        for name in self.plan[self.point] if self.point < len(self.plan) else (): self.step(name)
+        while self.jobs:
+            for name in list(self.jobs): self.step(name)
+
+def add_to(acc, inc):
+    acc[...] = (acc[...].astype(F32) + inc[...].astype(F32)).astype(BF)
+
+class Copies:
+    def __init__(self, sems): self.sems, self.n = sems, 0
+    def go(self, src, dst):
+        copy = pltpu.make_async_copy(src, dst, at(self.sems, self.n))
+        self.n += 1
+        copy.start()
+        return copy
+
+def turns(nz):
+    out, lo, hi = [], 0, nz - 1
+    while lo <= hi:
+        out += [hi, lo] if lo < hi else [lo]
+        lo, hi = lo + 1, hi - 1
+    return out
 
 def place():
     d = lax.axis_index("dp"); f = lax.axis_index("fsdp")
     return d, f, d // 2, d % 2, f // 2, f % 2
+
+def wide_barrier(nz):
+    d, f, z, y, x, c = place()
+    bar = pltpu.get_barrier_semaphore()
+    for dev in ((d, f ^ 1), (d, f ^ 2), (d, f ^ 3), (d ^ 1, f)):
+        pl.semaphore_signal(bar, inc=1, device_id=dev, device_id_type=MESH)
+    @pl.when(z > 0)
+    def _(): pl.semaphore_signal(bar, inc=1, device_id=(d - 2, f), device_id_type=MESH)
+    @pl.when(z < nz - 1)
+    def _(): pl.semaphore_signal(bar, inc=1, device_id=(d + 2, f), device_id_type=MESH)
+    pl.semaphore_wait(bar, 4 + (z > 0).astype(jnp.int32) + (z < nz - 1).astype(jnp.int32))
+
+D_PIECES = (("a", "yxz", 0, 384), ("b", "xyz", 384, 768))
+W_PIECES = (("p", "zyx", 1280, 1920), ("o", "xyz", 0, 1280))
+Q_PIECES = (("q", "yz", 0, 384), ("r", "zy", 384, 768))
+
+class Piece:
+    def __init__(self, name, order, rows, cols, nz, pair=True):
+        self.name, self.order, self.rows, self.cols, self.nz, self.pair = name, order, rows, cols, nz, pair
+        self.nx = 2 if pair else 1
+    def live(self, done):
+        return ((2,) if "y" not in done else ()) + ((self.nx,) if "x" not in done else ()) + (self.rows, self.cols)
+    def buffers(self):
+        out = {"acc": (self.nz, 2, self.nx, self.rows, self.cols)}
+        if self.pair: out["stg"] = out["sib"] = out["acc"]
+        done = ""
+        for axis in self.order:
+            if axis == "z": out["z"] = (2, self.nz) + self.live(done)
+            else: out[axis] = (() if "z" in done else (self.nz,)) + self.live(done + axis)
+            done += axis
+        return {self.name + k: (s, BF) for k, s in out.items()}
+    def bind(self, bufs, s):
+        self.s, self.net, self.agenda = s, s.net, s.agenda
+        self.b = {k[len(self.name):]: v for k, v in bufs.items() if k.startswith(self.name) and k[len(self.name):] in ("acc", "stg", "sib", "x", "y", "z")}
+        self.sems, self.flows, self.done = {}, 0, False
+        return self
+    def view(self, t, done, other=""):
+        s = self.s
+        ys = pl.ds(0, 2) if "y" not in done else 1 - s.y if other == "y" else s.y
+        xs = pl.ds(0, self.nx) if "x" not in done else 1 - s.x if other == "x" else s.x
+        return at(self.b["acc"], t, ys, xs)
+    def start(self, t):
+        if self.pair:
+            self.sems[t] = self.net.sem()
+            self.net.send(at(self.b["stg"], t), at(self.b["sib"], t), self.sems[t], self.s.sp)
+        self.agenda.add(self.name + str(t), self.plane(t))
+    def exchange(self, axis, t, done):
+        k = self.net.sem()
+        self.net.send(self.view(t, done + axis, axis), self.inbox(axis, t, done), k, self.s.xp if axis == "x" else self.s.yp)
+        return k
+    def inbox(self, axis, t, done):
+        return self.b[axis] if "z" in done else at(self.b[axis], t)
+    def plane(self, t):
+        if self.pair:
+            self.net.got(at(self.b["sib"], t), self.sems[t])
+            add_to(at(self.b["acc"], t), at(self.b["sib"], t))
+        done = ""
+        for axis in self.order:
+            if axis == "z": break
+            k = self.exchange(axis, t, done)
+            done += axis
+            yield
+            buf = self.inbox(axis, t, done)
+            self.net.got(buf, k)
+            add_to(self.view(t, done), buf)
+        yield from self.flow(t, done)
+        self.flows += 1
+        if self.flows == self.nz:
+            if self.order[-1] == "z": self.done = True
+            else: self.agenda.add(self.name + "e", self.rest())
+    def flow(self, t, done):
+        nz, s, ks, recv = self.nz, self.s, (self.net.sem(), self.net.sem()), self.b["z"]
+        far = max(t, nz - 1 - t)
+        for h in range(far):
+            if h: yield
+            for way, total, here, dev in ((0, t, s.is_z[h], s.up), (1, nz - 1 - t, s.is_z[nz - 1 - h], s.down)):
+                if h < total:
+                    inc = at(recv, way, t)
+                    if h:
+                        self.net.got(inc, ks[way], here)
+                        pl.when(here)(lambda inc=inc: add_to(self.view(t, done), inc))
+                    self.net.send(self.view(t, done), inc, ks[way], dev, here)
+        yield
+        if t > 0: self.net.got(at(recv, 0, t), ks[0], s.is_z[t])
+        if t < nz - 1: self.net.got(at(recv, 1, t), ks[1], s.is_z[t])
+    def rest(self):
+        s, i = self.s, self.order.index("z")
+        done = self.order[:i + 1]
+        own = self.view(s.z, done)
+        for pred, way in ((s.has_below, 0), (s.has_above, 1)):
+            pl.when(pred)(lambda way=way: add_to(own, at(self.b["z"], way, s.z)))
+        for axis in self.order[i + 1:]:
+            k = self.exchange(axis, s.z, done)
+            done += axis
+            yield
+            buf = self.inbox(axis, s.z, done)
+            self.net.got(buf, k)
+            if axis != self.order[-1]: add_to(self.view(s.z, done), buf)
+        self.done = True
+    def total(self):
+        assert self.done
+        s, last = self.s, self.order[-1]
+        sum_ = self.b["acc"][s.z, s.y, s.x if self.pair else 0].astype(F32)
+        if last != "z": return sum_ + self.b[last][...].astype(F32).reshape(sum_.shape)
+        for pred, way in ((s.has_below, 0), (s.has_above, 1)):
+            sum_ = sum_ + jnp.where(pred, self.b["z"][way, s.z].astype(F32).reshape(sum_.shape), 0.0)
+        return sum_
+
+class Sums:
+    def __init__(self, nz, net, agenda, bufs, outs, vin):
+        self.nz, self.net, self.agenda, self.b, self.o, self.vin = nz, net, agenda, bufs, outs, vin
+        self.d, self.f, self.z, self.y, self.x, self.c = place()
+        d, f = self.d, self.f
+        self.up, self.down = (d + 2, f), (d - 2, f)
+        self.yp, self.xp, self.sp = (d ^ 1, f), (d, f ^ 2), (d, f ^ 1)
+        self.turn = turns(nz)
+        z = self.z
+        self.is_z = [z == h for h in range(nz)]
+        self.has_below, self.has_above, self.core0 = z > 0, z < nz - 1, self.c == 0
+        self.D, self.W, self.Q = [[p.bind(bufs, self) for p in ps] for ps in pieces(nz)]
+    def first(self, v): return jnp.where(self.core0, v[0], v[1])
+    def second(self, v): return jnp.where(self.core0, v[1], v[0])
+    def cols(self, ref, width, off, n, mine, rows=None):
+        cc = self.c if mine else 1 - self.c
+        return ref[slice(None) if rows is None else rows, pl.ds(pl.multiple_of(cc * width + off, 128), n)]
+
+    def vectors(self):
+        net, b, z, nz = self.net, self.b, self.z, self.nz
+        vb, vr, hop = b["vb"], b["vr"], b["hop"]
+        vb[...] = self.vin()
+        for i, dev in enumerate((self.sp, self.xp, self.yp)):
+            k = net.sem()
+            hop[i] = vb[...]
+            net.send(at(hop, i), at(vr, i), k, dev)
+            yield
+            net.got(at(vr, i), k)
+            vb[...] += vr[i]
+        for i in (3, 4): hop[i] = vb[...]
+        ks = [net.sem(), net.sem()]
+        for step in range(nz - 1):
+            if step: yield
+            for way, here, dev in ((0, self.is_z[step], self.up), (1, self.is_z[nz - 1 - step], self.down)):
+                if step:
+                    net.got(at(vr, 3 + way), ks[way], here)
+                    @pl.when(here)
+                    def _(way=way): hop[3 + way] += vr[3 + way]
+                net.send(at(hop, 3 + way), at(vr, 3 + way), ks[way], dev, here)
+        yield
+        for way, last, some in ((0, self.is_z[nz - 1], self.has_below), (1, self.is_z[0], self.has_above)):
+            net.got(at(vr, 3 + way), ks[way], last)
+            @pl.when(some)
+            def _(way=way): vb[...] += vr[3 + way]
+        self.o["v"][...] = vb[...]
+
+    def down_tile(self, t, g):
+        g = g.reshape(2, 2, 2, 96, D)
+        for p, (_, _, c0, c1) in zip(self.D, D_PIECES):
+            for y in range(2):
+                for x in range(2):
+                    p.b["acc"][t, y, x] = self.first(g[y, x, :, :, c0:c1]).astype(BF)
+                    p.b["stg"][t, y, x] = self.second(g[y, x, :, :, c0:c1]).astype(BF)
+            p.start(t)
+    def wide_piece(self, p, c0, c1, n2, du, og, da):
+        for dst, mine in (("acc", True), ("stg", False)):
+            if c0 < 384:
+                n = min(c1, 384) - c0
+                for j in range(4):
+                    g = sum(tn(og[k, j, :, 0:192], self.cols(da, 384, c0, n, mine, pl.ds(k * T, T))) for k in range(2))
+                    p.b[dst][j * self.nz // 4:(j + 1) * self.nz // 4, :, :, :, 0:n] = g.astype(BF).reshape(self.nz // 4, 2, 2, 48, n)
+            if c1 > 384:
+                lo = max(c0, 384)
+                g = tn(n2[...], self.cols(du, 1536, lo - 384, c1 - lo, mine))
+                p.b[dst][:, :, :, :, lo - c0:c1 - c0] = g.astype(BF).reshape(self.nz, 2, 2, 48, c1 - lo)
+        for t in self.turn: p.start(t)
+    def q_piece(self, p, c0, c1, n1s, dqs):
+        for j in range(2):
+            g = sum(tn(n1[:, j * 384:(j + 1) * 384], dq[:, c0:c1]) for n1, dq in zip(n1s, dqs))
+            p.b["acc"][j * self.nz // 2:(j + 1) * self.nz // 2] = g.astype(BF).reshape(self.nz // 2, 2, 1, 96, c1 - c0)
+        for t in self.turn: p.start(t)
+    def ends(self):
+        net, half, c, f, qf = self.net, self.b["half"], self.c, self.f, self.b["qf"]
+        for p, (_, _, c0, c1) in zip(self.W, W_PIECES):
+            total = p.total()
+            half[0, :, c0:c1] = self.first((total[0:24], total[24:48]))
+            half[1, :, c0:c1] = self.second((total[0:24], total[24:48]))
+        kw = net.sem()
+        net.send(at(half, 1), at(half, 2), kw, self.sp)
+        for p, (_, _, c0, c1) in zip(self.Q, Q_PIECES):
+            total = p.total()
+            for j in range(4): qf[0, j, :, c0:c1] = total[j * 24:(j + 1) * 24]
+        ks = [net.sem() for _ in range(4)]
+        for k in (1, 2, 3):
+            net.send(at(qf, 0, f ^ k), at(qf, 1, f), ks[k], (self.d, f ^ k))
+        self.o["qkv"][f] = qf[0, f]
+        for p, (_, _, c0, c1) in zip(self.D, D_PIECES):
+            self.o["down"][:, c0:c1] = p.total()
+        net.got(at(half, 2), kw)
+        for cc, s in ((c, 0), (1 - c, 2)):
+            self.o["outw"][:, pl.ds(pl.multiple_of(cc * 384, 128), 384)] = half[s, :, 0:384]
+            self.o["up"][:, pl.ds(pl.multiple_of(cc * 1536, 128), 1536)] = half[s, :, 384:1920]
+        for k in (1, 2, 3):
+            net.got(at(qf, 1, f ^ k), ks[k])
+            self.o["qkv"][f ^ k] = qf[1, f ^ k]
+
+def pieces(nz):
+    return ([Piece(n, o, 96, c1 - c0, nz) for n, o, c0, c1 in D_PIECES], [Piece(n, o, 48, c1 - c0, nz) for n, o, c0, c1 in W_PIECES],
+            [Piece(n, o, 96, c1 - c0, nz, False) for n, o, c0, c1 in Q_PIECES])
+
+def sum_buffers(nz):
+    out = dict(qf=((2, 4, 24, D), F32), hop=((5, 8, D), F32), half=((3, 24, 1920), F32), vb=((8, D), F32), vr=((5, 8, D), F32))
+    for group in pieces(nz):
+        for p in group: out.update(p.buffers())
+    return out
+
+def bwd_kernel(last, nz, names, *refs):
+    r_ = dict(zip(names, refs))
+    R = lambda *ns: [r_[n] for n in ns]
+    lim, vec, g_h, x_h, wq_h, wou_h, wd_h, qkv_h, o_h, lse_h, r_h, gp_h = R("lim", "vec", "g", "x", "wq", "wou", "wd", "qkv", "o", "lse", "r", "gp")
+    dos, do, mine, part, inc, go, dr, dqkv, sums, bsum = R("dos", "do", "mine", "part", "inc", "go_v", "dr", "dqkv_v", "sums", "bsum")
+    d = lax.axis_index("dp"); f = lax.axis_index("fsdp")
+    ZERO[0] = f * 0
+    mem = Copies(r_["lsem"])
+    net = Links(r_["ssem"], r_["rsem"], (d, f ^ 1))
+    agenda = Agenda(PLAN if last and nz == 4 else ())
+    limit = lim[0]
+    g0, g1, emb = vec[0:1, :], vec[1:2, :], vec[2:3, :]
+    W = 768
+    V = pltpu.VMEM
+    N = 2 * T if last else T
+    if last:
+        gs = Sums(nz, net, agenda, r_, dict(v=r_["v_o"], down=r_["down_o"], outw=r_["outw_o"], up=r_["up_o"], qkv=r_["qkv_o"]), None)
+        sums1, bsum1 = r_["sums_1"], r_["bsum_1"]
+        def all_sums():
+            bias = [bsum[:, j * D:(j + 1) * D] + bsum1[:, j * D:(j + 1) * D] for j in range(4)]
+            return jnp.concatenate([sums[0:2, :] + sums1[0:2, :], sums[2:3, :], sums1[2:3, :]] + bias, axis=0)
+        gs.vin = all_sums
+    g_in = mem.go(g_h, dr)
+    sums[...] = jnp.zeros_like(sums)
+
+    def phase1(du, dm, da):
+        def phase1a(a, wd, gp):
+            lw, lg = mem.go(wd_h, wd), mem.go(gp_h, gp)
+            if last:
+                la = [mem.go(r_["a_0"], at(a, pl.ds(0, T))), mem.go(r_["a_1"], at(a, pl.ds(T, T))), mem.go(r_["dm_1"], at(dm, pl.ds(T, T)))]
+                late = [mem.go(r_["du_1"], at(du, pl.ds(T, T))), mem.go(r_["da_1"], at(da, pl.ds(T, T)))]
+            if last: wide_barrier(nz)
+            else: group_barrier(d, f)
+            g_in.wait()
+            dm[0:T, :] = dr[...].astype(BF)
+            if last:
+                for c in la: c.wait()
+                for t in gs.turn:
+                    gs.down_tile(t, tn(a[:, t * W:(t + 1) * W], dm[...]))
+                    agenda.run()
+            out = [] if last else [mem.go(dm, r_["dm_o"])]
+            lw.wait(); lg.wait()
+            for j in range(FF // W):
+                cols = pl.ds(j * W, W)
+                t = (nt(dm[0:T, :], wd[cols, :]) * gp[:, cols].astype(F32)).astype(BF)
+                du[0:T, cols] = t
+                bsum[:, cols] = jnp.sum(t.astype(F32), axis=0, keepdims=True)
+                agenda.run()
+            if not last: out.append(mem.go(du, r_["du_o"]))
+            for c in out: c.wait()
+            if last:
+                for c in late: c.wait()
+        if last: pl.run_scoped(phase1a, V((N, FF), BF), V((FF, D), BF), V((T, FF), BF))
+        else: pl.run_scoped(partial(phase1a, None), V((FF, D), BF), V((T, FF), BF))
+
+        def phase1b(wou, r, n2, og):
+            lr, lw = mem.go(r_h, r), mem.go(wou_h, wou)
+            if last:
+                late = [mem.go(r_["n2_0"], at(n2, pl.ds(0, T))), mem.go(r_["n2_1"], at(n2, pl.ds(T, T))), mem.go(r_["og_0"], at(og, 0)), mem.go(r_["og_1"], at(og, 1))]
+            lr.wait(); lw.wait()
+            def norm2(j, _):
+                rows = rows_at(j * 128, 128)
+                e = nt(du[rows, :], wou[:, D:])
+                xhat, scale = normed(r[rows, :])
+                sums[1:2, :] += jnp.sum(e * xhat, axis=0, keepdims=True)
+                t = dr[rows, :] + norm_back(xhat, scale, e, g1)
+                dr[rows, :] = t
+                da[rows, :] = t.astype(BF)
+                return 0
+            lax.fori_loop(0, T // 128, norm2, 0)
+            out = [] if last else [mem.go(da, r_["da_o"])]
+            for k in (3, 2, 1, 0):
+                b = f ^ k
+                dos[b, :, 0:192] = nt(da[0:T, :], wou[rows_at(b * 192, 192), 0:D]).astype(BF)
+                dos[b, :, 192:256] = jnp.zeros((T, 64), BF)
+                if k: net.send(at(dos, b), at(do, rows_at(f * T, T)), do_sems[k], (d, b))
+                else: do[rows_at(f * T, T), :] = dos[b]
+            if last:
+                agenda.run()
+                for c in late: c.wait()
+                for p, (_, _, c0, c1) in zip(gs.W, W_PIECES):
+                    gs.wide_piece(p, c0, c1, n2, du, og, da)
+                    agenda.run()
+            for c in out: c.wait()
+        if last: pl.run_scoped(phase1b, V((D, 3840), BF), V((T, D), F32), V((N, D), BF), V((2, 4, T, 256), BF))
+        else: pl.run_scoped(lambda w, r: phase1b(w, r, None, None), V((D, 3840), BF), V((T, D), F32))
+    do_sems = [net.sem() for _ in range(4)]
+    pl.run_scoped(phase1, V((N, FF), BF), V((N, D), BF), V((N, D), BF))
+
+    def phase2(qkv, o, lse, qT, kT, doT, dqT, delta, dkv):
+        loads = [mem.go(*p) for p in ((qkv_h, qkv), (o_h, o), (lse_h, lse))]
+        dkv[...] = jnp.zeros_like(dkv)
+        dqT[192:256, :] = jnp.zeros((64, S), F32)
+        agenda.run()
+        for c in loads: c.wait()
+        qT[...] = (qkv[:, 0:256] * 0.125).astype(BF).T
+        kT[...] = qkv[:, 256:512].T
+        agenda.run(hold=True)
+        for k in (1, 2, 3): net.got(at(do, rows_at((f ^ k) * T, T)), do_sems[k])
+        doT[...] = do[...].T
+        prod = (do[...].astype(F32) * o[...].astype(F32)).T
+        for h in range(3):
+            delta[h:h + 1, :] = jnp.sum(prod[h * 64:h * 64 + 64], axis=0, keepdims=True)
+        for i in range(S // QB):
+            for kc in range(i + 1):
+                for h in range(3):
+                    bwd_block(i, kc, h, qkv, do, lse, limit, qT, kT, doT, dqT, delta, dkv)
+                    agenda.run()
+        dqkv[:, 0:256] = (dqT[...] * 0.125).astype(BF).T
+        dqkv[:, 256:512] = (dkv[:, 0:256] * 0.125).astype(BF)
+        dqkv[:, 512:768] = dkv[:, 256:512].astype(BF)
+    pl.run_scoped(phase2, V((S, D), BF), V((S, 256), BF), V((8, S), F32), V((256, S), BF), V((256, S), BF), V((256, S), BF), V((256, S), F32), V((8, S), F32), V((S, 512), F32))
+
+    def phase3(wq, x, n1a, n1b, dq1):
+        lw, lx = mem.go(wq_h, wq), mem.go(x_h, x)
+        if last:
+            late = [mem.go(r_["n1_0"], n1a), mem.go(r_["n1_1"], n1b), mem.go(r_["dq_1"], dq1)]
+        out = [] if last else [mem.go(dqkv, r_["dqkv_o"])]
+        lw.wait()
+        def partial_rows(b, j):
+            return nt(dqkv[rows_at(b * T + j * CH, CH), :], wq[...])
+        k0, k1, k2 = [[net.sem() for _ in range(3)] for _ in range(3)]
+        for j in range(3):
+            rows = pl.ds(j * CH, CH)
+            mine[0, rows, :] = partial_rows(f ^ 3, j).astype(BF)
+            net.send(at(mine, 0, rows), at(part, 0, rows), k0[j], (d, f ^ 1))
+        for j in range(3):
+            rows = pl.ds(j * CH, CH)
+            t = partial_rows(f ^ 2, j)
+            agenda.run(hold=True)
+            net.got(at(part, 0, rows), k0[j])
+            inc[rows, :] = (t + part[0, rows, :].astype(F32)).astype(BF)
+            net.send(at(inc, rows), at(part, 2, rows), k2[j], (d, f ^ 2))
+        for j in range(3):
+            rows = pl.ds(j * CH, CH)
+            mine[1, rows, :] = partial_rows(f ^ 1, j).astype(BF)
+            net.send(at(mine, 1, rows), at(part, 1, rows), k1[j], (d, f ^ 1))
+        for j in range(3):
+            rows = pl.ds(j * CH, CH)
+            go[rows, :] = partial_rows(f, j)
+        lx.wait()
+        def finish_rows():
+            for j in range(3):
+                rows = pl.ds(j * CH, CH)
+                net.got(at(part, 1, rows), k1[j])
+                net.got(at(part, 2, rows), k2[j])
+                e = go[rows, :] + part[1, rows, :].astype(F32) + part[2, rows, :].astype(F32)
+                xhat, scale = normed(x[rows, :].astype(F32) + emb)
+                sums[0:1, :] += jnp.sum(e * xhat, axis=0, keepdims=True)
+                t = dr[rows, :] + norm_back(xhat, scale, e, g0)
+                sums[2:3, :] += jnp.sum(t, axis=0, keepdims=True)
+                go[rows, :] = t
+                if j < 2: yield
+            out.append(mem.go(go, r_["go_o"]))
+            if last: agenda.add("V", gs.vectors())
+        agenda.add("G", finish_rows())
+        if last:
+            agenda.run()
+            for c in late: c.wait()
+            for p, (_, _, c0, c1) in zip(gs.Q, Q_PIECES):
+                gs.q_piece(p, c0, c1, (n1a, n1b), (dqkv, dq1))
+                agenda.run()
+        agenda.finish()
+        if last:
+            gs.ends()
+        for c in out: c.wait()
+    if last: pl.run_scoped(phase3, V((D, D), BF), V((T, D), F32), V((S, D), BF), V((S, D), BF), V((S, D), BF))
+    else: pl.run_scoped(lambda w, x: phase3(w, x, None, None, None), V((D, D), BF), V((T, D), F32))
+    net.close()
+
+def bwd(lim, g, x, vec, wq, wou, wd, kept, cid, last=None, nz=None):
+    n1, qkv, o, lse, og, r, n2, gp, a = kept
+    hbm = pl.BlockSpec(memory_space=pltpu.HBM); vm = pl.BlockSpec(memory_space=pltpu.VMEM); sm = pl.BlockSpec(memory_space=pltpu.SMEM)
+    ins = dict(lim=lim, vec=vec, g=g, x=x, wq=wq, wou=wou, wd=wd, qkv=qkv, o=o, lse=lse, r=r, gp=gp)
+    outs = dict(go_o=((T, D), F32), sums=((8, D), F32), bsum=((1, FF), F32))
+    if last is None:
+        outs.update(dm_o=((T, D), BF), du_o=((T, FF), BF), da_o=((T, D), BF), dqkv_o=((S, D), BF))
+    else:
+        ins.update(last)
+        ins.update(a_0=a, n2_0=n2, og_0=og, n1_0=n1)
+        outs.update(down_o=((96, D), F32), outw_o=((24, D), F32), up_o=((24, FF), F32), qkv_o=((4, 24, D), F32), v_o=((8, D), F32))
+    scratch = dict(dos=((4, T, 256), BF), do=((S, 256), BF), mine=((2, T, D), BF), part=((3, T, D), BF), inc=((T, D), BF), go_v=((T, D), F32), dr=((T, D), F32), dqkv_v=((S, D), BF))
+    if last is not None: scratch.update(sum_buffers(nz))
+    sems = 320 if last is not None else 16
+    names = list(ins) + list(outs) + list(scratch) + ["lsem", "ssem", "rsem"]
+    place_of = lambda n: sm if n == "lim" else vm if n in ("vec", "sums", "bsum", "sums_1", "bsum_1", "down_o", "outw_o", "up_o", "qkv_o", "v_o") else hbm
+    res = pl.pallas_call(partial(bwd_kernel, last is not None, nz, names),
+        out_shape=[jax.ShapeDtypeStruct(*s) for s in outs.values()],
+        in_specs=[place_of(n) for n in ins], out_specs=[place_of(n) for n in outs],
+        scratch_shapes=[pltpu.VMEM(*s) for s in scratch.values()] + [pltpu.SemaphoreType.DMA((32,)), pltpu.SemaphoreType.DMA((sems,)), pltpu.SemaphoreType.DMA((sems,))],
+        compiler_params=pltpu.CompilerParams(collective_id=cid, has_side_effects=True, vmem_limit_bytes=VMEM_LIMIT))(*ins.values())
+    return dict(zip(outs, res))
 
 def gather_kernel(nz, q4, ou, dn, wq, wou, we, wd, rq, rou, blk, blkq, local, ssem, rsem):
     d, f, z, y, x, c = place()
@@ -507,28 +876,39 @@
             pltpu.SemaphoreType.DMA((4,)), pltpu.SemaphoreType.DMA((NSEM,)), pltpu.SemaphoreType.DMA((NSEM,))],
         compiler_params=pltpu.CompilerParams(collective_id=0, has_side_effects=True, vmem_limit_bytes=32 * 2**20))(q4, ou, dn)
 
-
 def gather_any(q4, ou, dn):
     both = ("dp", "fsdp")
     mine = lax.dynamic_index_in_dim(lax.all_gather(q4, both, axis=0), lax.axis_index("fsdp"), 1, keepdims=False)
     full = lax.all_gather(ou, both, axis=0, tiled=True)
     return mine.reshape(D, D), full[:, :3840], full[:, 3840:], lax.all_gather(dn, both, axis=0, tiled=True)
 
+def grads_any(kept0, kept1, vin, rd):
+    both = ("dp", "fsdp")
+    a, dm, n2, du, og, da, n1, dq = [jnp.concatenate([u, v], axis=0) for u, v in zip(kept0, kept1)]
+    heads = og.reshape(2, 4, T, 256)[..., :192].transpose(0, 2, 1, 3).reshape(2 * T, D)
+    scatter = lambda v: lax.psum_scatter(v, both, scatter_dimension=0, tiled=True)
+    q = tn(n1, dq).reshape(1, D // rd, rd, D)
+    q = lax.dynamic_update_slice(jnp.zeros((4, D // rd, rd, D), F32), q, (lax.axis_index("fsdp"), 0, 0, 0))
+    q_grad = lax.psum_scatter(q, both, scatter_dimension=1, tiled=True).reshape(4, rd, D)
+    return scatter(tn(a, dm)), scatter(tn(heads, da)), scatter(tn(n2, du)), q_grad, lax.psum(vin, both)
+
 def body(tokens, qkv_weight, out_weight, up_weight, down_weight, norm_gains, up_bias, pass_table, pass_index, lengths, cotangent):
     rd = qkv_weight.shape[0]
+    nz = lax.axis_size("dp") // 2
+    f = lax.axis_index("fsdp")
     q4 = jnp.pad(qkv_weight.reshape(rd, 3, 4, 192), ((0, 0), (0, 0), (0, 0), (0, 64))).transpose(2, 0, 1, 3).reshape(4, rd, D)
     chooser = [(jnp.arange(pass_table.shape[1], dtype=jnp.int32) == pass_index[n]).astype(F32) for n in range(2)]
     emb = jnp.stack([jnp.sum(pass_table.astype(F32) * ch[None, :], axis=1) for ch in chooser], axis=1).astype(BF)
     e = jnp.concatenate([norm_gains, emb, up_bias.reshape(rd, 4), jnp.zeros((rd, 120), BF)], axis=1)
     ou = jnp.concatenate([out_weight, up_weight, e], axis=1)
     if rd == 24:
-        wq, wou, we, wd = gather(q4, ou, down_weight, lax.axis_size("dp") // 2)
+        wq, wou, we, wd = gather(q4, ou, down_weight, nz)
     else:
         wq, wou, we, wd = gather_any(q4, ou, down_weight)
     vecs = we[:, 0:4].T.astype(F32)
     vec = [jnp.concatenate([vecs[0:2], vecs[2 + n:3 + n], jnp.zeros((5, D), F32)], axis=0) for n in range(2)]
     bias = we[:, 4:8].reshape(1, FF).astype(F32)
-    row_pos = lax.axis_index("fsdp") * T + jnp.arange(T, dtype=jnp.int32)
+    row_pos = f * T + jnp.arange(T, dtype=jnp.int32)
     valid = (row_pos < lengths[0]).astype(F32)[:, None]
     xs = [tokens.astype(F32)]; kept = []
     for n in range(2):
@@ -536,28 +916,26 @@
         xs.append(res[0]); kept.append(res[1:])
     block_out = (xs[2] * valid).astype(BF)
     g = cotangent.astype(F32) * valid
-    grads = [None, None]; sums = [None, None]; bs = [None, None]
-    for n in (1, 0):
-        n1, qkv, o, lse, og, r, n2, gp, a = kept[n]
-        g, dm, du, da, dqkv, sums[n], bs[n] = bwd(lengths, g, xs[n], vec[n], wq, wou, wd, qkv, o, lse, r, gp, 2)
-        grads[n] = (a, dm, n2, du, og, da, n1, dqkv)
-    tn = lambda a, b: lax.dot_general(a, b, (((0,), (0,)), ((), ())), preferred_element_type=F32)
-    cat = lambda i, sh: jnp.concatenate([grads[0][i].reshape(sh), grads[1][i].reshape(sh)], axis=0)
-    a, dm, n2, du = cat(0, (T, FF)), cat(1, (T, D)), cat(2, (T, D)), cat(3, (T, FF))
-    og = jnp.concatenate([grads[n][4][:, :, :192].transpose(1, 0, 2).reshape(T, D) for n in range(2)], axis=0)
-    da, n1, dqkv = cat(5, (T, D)), cat(6, (S, D)), cat(7, (S, D))
-    down_grad = tn(a, dm); up_grad = tn(n2, du); out_grad = tn(og, da); qg = tn(n1, dqkv)
-    ps = lambda v: lax.psum_scatter(v, ("dp", "fsdp"), scatter_dimension=0, tiled=True)
-    f = lax.axis_index("fsdp")
-    qg = qg.reshape(D, 3, 256)[:, :, :192]
-    full = lax.dynamic_update_slice(jnp.zeros((D, 3, D), F32), qg, (0, 0, f * 192)).reshape(D, 3 * D)
-    tot = lax.psum((sums[0], sums[1], bs[0] + bs[1]), ("dp", "fsdp"))
+    b1 = bwd(lengths, g, xs[1], vec[1], wq, wou, wd, kept[1], 2)
+    n1, qkv, o, lse, og, r, n2, gp, a = kept[1]
+    if rd == 24:
+        left = dict(a_1=a, dm_1=b1["dm_o"], n2_1=n2, du_1=b1["du_o"], og_1=og, da_1=b1["da_o"], n1_1=n1.reshape(S, D), dq_1=b1["dqkv_o"], sums_1=b1["sums"], bsum_1=b1["bsum"])
+        mine = (kept[0][0].reshape(S, D),) + tuple(kept[0][1:])
+        b0 = bwd(lengths, b1["go_o"], xs[0], vec[0], wq, wou, wd, mine, 3, left, nz)
+        down_grad, out_grad, up_grad, q_grad, tot = b0["down_o"], b0["outw_o"], b0["up_o"], b0["qkv_o"], b0["v_o"]
+    else:
+        b0 = bwd(lengths, b1["go_o"], xs[0], vec[0], wq, wou, wd, kept[0], 2)
+        groups = [(k[8], b["dm_o"], k[6], b["du_o"], k[4], b["da_o"], k[0].reshape(S, D), b["dqkv_o"]) for k, b in zip(kept, (b0, b1))]
+        s0, s1 = b0["sums"], b1["sums"]
+        vin = jnp.concatenate([s0[0:2] + s1[0:2], s0[2:3], s1[2:3], (b0["bsum"] + b1["bsum"]).reshape(4, D)], axis=0)
+        down_grad, out_grad, up_grad, q_grad, tot = grads_any(*groups, vin, rd)
+    qkv_grad = q_grad.reshape(4, rd, 3, 256)[..., :192].transpose(1, 2, 0, 3).reshape(rd, 3 * D)
     idx = lax.axis_index("dp") * 4 + f
     own = lambda v: lax.dynamic_slice_in_dim(v, idx * rd, rd, 0)
-    gains = own(jnp.stack([tot[0][0] + tot[1][0], tot[0][1] + tot[1][1]], axis=1))
-    table = own(tot[0][2])[:, None] * chooser[0][None] + own(tot[1][2])[:, None] * chooser[1][None]
-    bias_grad = lax.dynamic_slice_in_dim(tot[2][0], idx * rd * 4, rd * 4, 0)
-    return (block_out, g, ps(full), ps(out_grad), ps(up_grad), ps(down_grad), gains, bias_grad, table)
+    gains = own(tot[0:2].T)
+    table = own(tot[2])[:, None] * chooser[0][None] + own(tot[3])[:, None] * chooser[1][None]
+    bias_grad = lax.dynamic_slice_in_dim(tot[4:8].reshape(FF), idx * rd * 4, rd * 4, 0)
+    return (block_out, b0["go_o"], qkv_grad, out_grad, up_grad, down_grad, gains, bias_grad, table)
 
 def solution(mesh):
     a = P(("dp", "fsdp"), None); b = P(("dp", "fsdp"))

time: 835 us -> 376 us (0.45)
  waiting for transfers between devices: 420 us -> 0 us
  Pallas kernels: 277 us -> 338 us
  blocking collectives: 39.8 us -> 0 us
  matrix products: 29.4 us -> 0 us
  local copies, waits for them, and re-layouts: 36.8 us -> 21.1 us
  between operations: 15.2 us -> 1.8 us
    reduce_scatter x3 -> x0, waiting for transfers between devices: 294 us -> none  [body(): lax.psum_scatter(v, ('dp', 'fsdp'), scatter_dimension=0, tiled=True)]
    unnamed x5 -> x0, waiting for transfers between devices: 125 us -> none
    pallas_call x2, Pallas kernels: 117 us -> 178 us  [bwd(): pl.pallas_call(partial(bwd_kernel, last is not None, nz, names), out_shap...]
    psum x1 -> x0, blocking collectives: 39.8 us -> none  [body(): tot = lax.psum((sums[0], sums[1], bs[0] + bs[1]), ('dp', 'fsdp'))]
    dot_general x4 -> x0, matrix products: 29.4 us -> none  [body(): lax.dot_general(a, b, (((0,), (0,)), ((), ())), preferred_element_type=F32)]
    unnamed x43 -> x29, local copies, waits for them, and re-layouts: 22.1 us -> 9.64 us
  transfers between devices with their start and end apart: 4 -> 0, of which waited for: 4 -> 0; matrix products, arithmetic and copies ran while one was open for 5% -> 0% of each run, Pallas kernels for 0% -> 0%
where the time goes in v3:
time: 376 us; the launch traced here: 368 us
  Pallas kernels  338 us (90%)
  local copies, waits for them, and re-layouts  21.1 us (6%)
  other arithmetic  7.3 us (2%)
    pallas_call x2, Pallas kernels, bwd(): pl.pallas_call(partial(bwd_kernel, last is not None, nz, names), out_shap...  178 us
    pallas_call x2, Pallas kernels, fwd(): pl.pallas_call(fwd_kernel, out_shape=[Z(*s) for s in outs], in_specs=[sm,...  91.8 us
    pallas_call x1, Pallas kernels, gather(): pl.pallas_call(partial(gather_kernel, nz), out_shape=(S((768, 768), BF),...  68.5 us
    unnamed x29, local copies, waits for them, and re-layouts  9.64 us

profile of v3, /device:TPU:1, one launch (start us, length us, event | category | flops | bytes accessed | tf_op | source)
XLA Modules:
  0.0 368.3 jit_solution(12870689845478005294)
XLA Ops:
  1.5 1.3 fusion.6
  2.8 1.3 compare_convert_fusion
  4.1 0.8 fusion.1
  5.1 0.7 copy.32
  5.8 0.7 reshape.81
  6.6 1.1 reshape.79
  8.2 1.1 convert_element_type.48.x.refs_3_
  9.3 68.5 %shard_map.178 = (bf16[768,768]{1,0:T(8,128)(2,1)S(1)}, bf16[768,3840]{1,0:T(8,128)(2,1)S(1)}, bf16[768,128]{1,0:T(8,128)(2,1)S(1)}, bf16[3072,768]{1,0:T(8,128)(2,1)S(1)}) custom-call(bf16[4,24,768]{2,1,0:T(8,128)(2,1)S(1)} %reshape.80.q4, bf16[24,3968]{1,0:T(8,128)(2,1)S(1)} %concatenate.10.ou, bf16[96,768]{1,0:T(8,128)(2,1)S(1)} %copy-done.3), custom_call_target="tpu_custom_call" | custom-call | tf_op jit(solution)/shard_map/pallas_call | solution.py:872
  77.8 2.5 copy-done
  80.3 2.2 copy-done.1
  82.5 1.0 copy-done.2
  85.1 0.9 reshape.87.bias
  86.0 43.7 %shard_map.179 = (f32[384,768]{1,0:T(8,128)}, bf16[4,384,768]{2,1,0:T(8,128)(2,1)}, bf16[1536,768]{1,0:T(8,128)(2,1)}, bf16[1536,256]{1,0:T(8,128)(2,1)}, f32[8,...) custom-call(s32[1]{0:T(128)} %copy.41.lim.refs_0_, ...), custom_call_target="tpu_custom_call" | custom-call | tf_op jit(solution)/shard_map/pallas_call | solution.py:213
  129.7 48.0 %shard_map.180 = (f32[384,768]{1,0:T(8,128)}, bf16[4,384,768]{2,1,0:T(8,128)(2,1)}, bf16[1536,768]{1,0:T(8,128)(2,1)}, bf16[1536,256]{1,0:T(8,128)(2,1)}, f32[8,...) custom-call(s32[1]{0:T(128)} %copy.41.lim.refs_0_, ...), custom_call_target="tpu_custom_call" | custom-call | tf_op jit(solution)/shard_map/pallas_call | solution.py:213
  177.8 2.7 convert_multiply_fusion
  180.5 64.0 %shard_map.181 = (f32[384,768]{1,0:T(8,128)}, f32[8,768]{1,0:T(8,128)}, f32[1,3072]{1,0:T(1,128)}, bf16[384,768]{1,0:T(8,128)(2,1)}, bf16[384,3072]{1,0:T(8,128)...) custom-call(s32[1]{0:T(128)} %copy.41.lim.refs_0_, f32[8,768]{1,0:T(8,128)} %maximum_maximum_fusion.vec.refs_1_, ...), custom_call_target="tpu_custom_call" | custom-call | tf_op jit(solution)/shard_map/pallas_call | solution.py:696
  244.4 113.9 %shard_map.182 = (f32[384,768]{1,0:T(8,128)}, f32[8,768]{1,0:T(8,128)}, f32[1,3072]{1,0:T(1,128)}, f32[96,768]{1,0:T(8,128)}, f32[24,768]{1,0:T(8,128)}, /*index...) custom-call(s32[1]{0:T(128)} %copy.41.lim.refs_0_, f32[8,768]{1,0:T(8,128)} %concatenate.11.vec.refs_1_, ...), custom_call_target="tpu_custom_call" | custom-call | tf_op jit(solution)/shard_map/pallas_call | solution.py:696
  358.3 0.7 slice.46
  359.7 0.8 fusion.5
  360.5 0.7 slice.47
  362.7 1.2 reshape.84
  364.2 0.9 reshape.85
  365.1 1.0 copy.42
  366.7 0.7 copy.44
  (48 shorter events, 6.0 us)
Async XLA Ops:
  0.6 7.4 %copy-start.9 = (bf16[24,3072]{1,0:T(8,128)(2,1)S(1)}, bf16[24,3072]{1,0:T(8,128)(2,1)}, u32[]{:S(2)}) copy-start(bf16[24,3072]{1,0:T(8,128)(2,1)} %param.14) | copy-start | bytes 442372
  0.7 7.4 %copy-start.11 = (bf16[24,768]{1,0:T(8,128)(2,1)S(1)}, bf16[24,768]{1,0:T(8,128)(2,1)}, u32[]{:S(2)}) copy-start(bf16[24,768]{1,0:T(8,128)(2,1)} %param.13) | copy-start | bytes 110596
  0.7 7.5 %copy-start.5 = (bf16[384,768]{1,0:T(8,128)(2,1)S(1)}, bf16[384,768]{1,0:T(8,128)(2,1)}, u32[]{:S(2)}) copy-start(bf16[384,768]{1,0:T(8,128)(2,1)} %param.11) | copy-start | bytes 1769476
  7.8 1.4 copy-start.3
  77.7 2.5 copy-start
  80.3 2.2 copy-start.1
  82.5 1.0 copy-start.2
  129.7 48.0 %copy-start.6 = (bf16[384,768]{1,0:T(8,128)(2,1)S(1)}, bf16[384,768]{1,0:T(8,128)(2,1)}, u32[]{:S(2)}) copy-start(bf16[384,768]{1,0:T(8,128)(2,1)} %param.21) | copy-start | bytes 1769476
  362.7 2.4 copy-start.4
  365.0 1.0 copy-start.10
  365.0 1.7 copy-start.8
  365.0 2.4 copy-start.7
